TPU v7x, 32 devices: a whole 2x2x4 slice. The times are simulated.
32 devices in a mesh: grp: 4 (over x, core), dev: 8 (over z, y).
Axes of the slice: x: 2, y: 2, z: 4, core: 2. Of those that a mesh axis runs over, the one named last changes fastest.
Arguments:
- residual: bfloat16 [4096, 2048], P(('grp', 'dev')), may hold values from -3 to 3
- queries: bfloat16 [4096, 1024], P(('grp', 'dev')), may hold values from -9 to 9
- keys: bfloat16 [4096, 256], P(('grp', 'dev')), may hold values from -6 to 6
- values: bfloat16 [4096, 256], P(('grp', 'dev')), may hold values from -18 to 18
- prefix_keys: bfloat16 [16, 512, 256], P('grp', 'dev'), may hold values from -6 to 6
- cached_prefix_values: bfloat16 [16, 512, 256], P('grp', 'dev'), may hold values from -18 to 18
- out_weight: bfloat16 [1024, 2048], replicated, may hold values from -0.1875 to 0.1875
- norm_gain: float32 [2048], replicated, may hold values from 0.25 to 1.75
- w_gate: bfloat16 [2048, 8192], P('grp', 'dev'), may hold values from -0.125 to 0.125
- w_up: bfloat16 [2048, 8192], P('grp', 'dev'), may hold values from -0.125 to 0.125
- w_down: bfloat16 [8192, 2048], P('dev', 'grp'), may hold values from -0.0625 to 0.0625
- suffix_lengths: int32 [4, 32], P('grp'), may hold values from 1 to 128, 1024 in all within a row
- request_group: int32 [4, 32], P('grp'), may hold values from 0 to 3, as said below
- placement_order: int32 [4, 32], P('grp'), may hold values from 0 to 31, each once within a row
Outputs:
- layer_out: bfloat16 [4096, 2048], P(('grp', 'dev'))
Inputs may be any that keep to these rules, and one draw needn't show every extreme that they name: `suffix_lengths`: the 32 lengths of one row sum to 1024. `request_group`: each row names each of its 4 groups exactly 8 times. `placement_order`: each row is an ordering of its 32 requests.
All inputs are finite; a program needn't handle non-finite values.
Results may differ from a plain program's by a relative error of at most 0.012.
Values may be sent and summed in bfloat16 or wider, within the bound.
No kernel may reach another device: no remote copies, remote signals or barrier semaphores. Data moves between devices by JAX's collectives and lax.ppermute only.
A program may use at most 128 MiB of HBM per device.

v0:
```python
import functools
import math

import jax
import jax.numpy as jnp
from jax import lax
from jax.experimental import pallas as pl
from jax.experimental.pallas import tpu as pltpu
from jax.sharding import PartitionSpec as P

HEAD_SIZE = 64
NEG_FILL = -1e30
EPSILON = 1e-05
F32 = jnp.float32
BF16 = jnp.bfloat16
LANES = 2 * HEAD_SIZE
CORES = 2
HALVES = 2


def cost(microseconds):
    return pl.CostEstimate(flops=0, bytes_accessed=int(microseconds * 3.5e6), transcendentals=0)


def dot(a, b, contract_b=0):
    return lax.dot_general(
        a, b, (((1,), (contract_b,)), ((), ())), preferred_element_type=F32
    )


def prepare_body(
    span,
    layout_hbm,
    queries_hbm,
    *refs,
):
    q_ref, before_ref, within_ref, prefix_ref = refs[:4]
    layout_ref, queries_ref, sems = refs[4:]
    copies = [
        pltpu.make_async_copy(source, target, sems.at[i])
        for i, (source, target) in enumerate(
            [
                (layout_hbm, layout_ref),
                (queries_hbm, queries_ref),
            ]
        )
    ]
    for copy in copies:
        copy.start()
    for copy in copies:
        copy.wait()
    tokens = queries_ref.shape[0]
    pairs, rows = q_ref.shape[0], q_ref.shape[1]
    per = rows // (2 * tokens)
    base = lax.axis_index("dev") * tokens
    own = base + lax.broadcasted_iota(jnp.int32, (tokens, LANES), 0)

    def request(k, carry):
        start, group, first = carry
        j = layout_ref[2, k]
        end = start + layout_ref[0, j]
        inside = (own >= start) & (own < end)
        return (
            end,
            jnp.where(inside, layout_ref[1, j], group),
            jnp.where(inside, start, first),
        )

    zero = jnp.zeros((tokens, LANES), jnp.int32)
    _, group, first = lax.fori_loop(0, layout_ref.shape[1], request, (jnp.int32(0), zero, zero))
    for ref, back in ((before_ref, tokens), (within_ref, 0)):
        for c in range(0, tokens, LANES):
            key = base - back + c + lax.broadcasted_iota(jnp.int32, (tokens, LANES), 1)
            ref[:, c : c + LANES] = jnp.where((key >= first) & (key <= own), 0.0, NEG_FILL)
    for c in range(0, prefix_ref.shape[1], LANES):
        key_group = lax.div(c + lax.broadcasted_iota(jnp.int32, (tokens, LANES), 1), span)
        prefix_ref[:, c : c + LANES] = jnp.where(group == key_group, 0.0, NEG_FILL)
    low = lax.broadcasted_iota(jnp.int32, (tokens, LANES), 1) < HEAD_SIZE
    for j in range(pairs):
        for parity in range(2):
            for r in range(per):
                head = (2 * j + parity) * per + r
                block = head // 2
                q = queries_ref[:, block * LANES : (block + 1) * LANES].astype(F32) * HEAD_SIZE ** (-0.5)
                if head % 2 != parity:
                    q = pltpu.roll(q, HEAD_SIZE, 1)
                q = jnp.where(low == (parity == 0), q, 0.0)
                row = (parity * per + r) * tokens
                q_ref[j, row : row + tokens, :] = q.astype(BF16)


def prepare(groups, span, lengths, request_group, packing, queries, width):
    tokens = queries.shape[0]
    layout = jnp.concatenate([lengths, request_group, packing], axis=0)
    per = queries.shape[1] // width
    vmem = pl.BlockSpec(memory_space=pltpu.VMEM)
    return pl.pallas_call(
        functools.partial(prepare_body, span),
        out_shape=[
            jax.ShapeDtypeStruct((width // LANES, 2 * per * tokens, LANES), BF16),
            jax.ShapeDtypeStruct((tokens, tokens), F32),
            jax.ShapeDtypeStruct((tokens, tokens), F32),
            jax.ShapeDtypeStruct((tokens, groups * span), F32),
        ],
        in_specs=[pl.BlockSpec(memory_space=pltpu.HBM)] * 2,
        out_specs=[vmem] * 4,
        compiler_params=pltpu.CompilerParams(vmem_limit_bytes=8 * 2**20),
        scratch_shapes=[
            pltpu.SMEM(layout.shape, jnp.int32),
            pltpu.VMEM(queries.shape, BF16),
            pltpu.SemaphoreType.DMA((2,)),
        ],
        cost_estimate=cost(3),
        name="prepare",
    )(layout, queries)


def attend_body(first, pieces, refs):
    q_ref, refs = refs[0], refs[1:]
    if not first:
        old_max, old_sum, old_acc = refs[:3]
        refs = refs[3:]
    kv = refs[: 3 * pieces]
    new_max, new_sum, new_acc = refs[-3:]
    pairs, rows = q_ref.shape[0], q_ref.shape[1]
    half = rows // 2
    low = lax.broadcasted_iota(jnp.int32, (half, LANES), 1) < HEAD_SIZE

    def pick(even, odd):
        return jnp.where(low, even, odd)

    for j in range(pairs):
        q = q_ref[j]
        lanes = slice(j * LANES, (j + 1) * LANES)
        scores = []
        for i in range(pieces):
            k_ref, bias_ref = kv[3 * i], kv[3 * i + 2]
            s = dot(q, k_ref[:, lanes], 1)
            keys = s.shape[1]
            bias = bias_ref[...]
            s = s.reshape(rows // bias.shape[0], bias.shape[0], keys) + bias[None]
            scores.append(s.reshape(rows, keys))
        top = functools.reduce(
            jnp.maximum, [jnp.max(s, axis=1, keepdims=True) for s in scores]
        )
        if first:
            row_max = top
            pair_max = pick(row_max[:half], row_max[half:])
        else:
            old = old_max[j]
            pair_max = jnp.maximum(old, pick(top[:half], top[half:]))
            row_max = jnp.concatenate(
                [pair_max[:, :1], pair_max[:, HEAD_SIZE : HEAD_SIZE + 1]], axis=0
            )
        total = None
        for i in range(pieces):
            v_ref = kv[3 * i + 1]
            w = jnp.exp(scores[i] - row_max).astype(BF16)
            v = v_ref[:, lanes]
            v = jnp.concatenate([v, jnp.ones_like(v)], axis=1)
            part = dot(w, v)
            total = part if total is None else total + part
        acc = pick(total[:half, :LANES], total[half:, :LANES])
        summed = pick(total[:half, LANES:], total[half:, LANES:])
        if not first:
            scale = jnp.exp(old - pair_max)
            acc = acc + scale * old_acc[j]
            summed = summed + scale * old_sum[j]
        new_max[j] = pair_max
        new_sum[j] = summed
        new_acc[j] = acc


def block_refs(refs, count):
    return [r for i in range(count) for r in (refs[2 * i].at[0], refs[2 * i].at[1], refs[2 * i + 1])]


def attend(q, state, blocks):
    pairs, rows, lanes = q.shape
    first = state is None

    def kernel(*refs):
        lead = 1 + (0 if first else 3)
        attend_body(first, len(blocks), [*refs[:lead], *block_refs(refs[lead:], len(blocks)), *refs[-3:]])

    shape = jax.ShapeDtypeStruct((pairs, rows // 2, lanes), F32)
    operands = [q] + ([] if first else list(state)) + [a for block in blocks for a in block]
    vmem = pl.BlockSpec(memory_space=pltpu.VMEM)
    return pl.pallas_call(
        kernel,
        out_shape=[shape] * 3,
        in_specs=[vmem] * len(operands),
        out_specs=[vmem] * 3,
        compiler_params=pltpu.CompilerParams(vmem_limit_bytes=(8 + 3 * len(blocks)) * 2**20),
        cost_estimate=cost(1.1 * len(blocks)),
        name="attend",
    )(*operands)


def block_owner(blocks, step):
    chips = blocks // CORES
    me = lax.axis_index("grp")
    x, core = lax.div(me, CORES), lax.rem(me, CORES)
    x = lax.rem(x + chips - step // CORES, chips)
    return x * CORES + lax.rem(core + step % CORES, CORES)


def project_body(
    blocks, sum_ref, acc_ref, weight_ref, residual_ref, gain_ref, hidden_ref, normed_refs, held
):
    pairs, rows, lanes = acc_ref.shape
    tokens = residual_ref.shape[0]
    per = rows // tokens
    hidden = residual_ref[...].astype(F32)
    for j in range(pairs):
        out = (acc_ref[j] / sum_ref[j]).astype(BF16)
        for r in range(0, per, 2):
            left = jnp.concatenate(
                [out[r * tokens : (r + 1) * tokens], out[(r + 1) * tokens : (r + 2) * tokens]], axis=1
            )
            heads = [(2 * j) * per + r, (2 * j + 1) * per + r, (2 * j) * per + r + 1, (2 * j + 1) * per + r + 1]
            right = jnp.concatenate(
                [weight_ref[h * HEAD_SIZE : (h + 1) * HEAD_SIZE, :] for h in heads], axis=0
            )
            hidden = hidden + dot(left, right)
    hidden_ref[...] = hidden
    mean = jnp.mean(hidden * hidden, axis=1, keepdims=True)
    held[...] = hidden * lax.rsqrt(mean + EPSILON) * gain_ref[...]
    width = hidden.shape[1] // blocks
    for b in range(blocks):
        start = pl.multiple_of(block_owner(blocks, b) * width, width)
        half, place = divmod(b, blocks // HALVES)
        normed_refs[half][:, place * width : (place + 1) * width] = held[:, pl.ds(start, width)].astype(BF16)


def attend_project(q, state, blocks, columns, out_weight, residual, gain):
    pairs, rows, lanes = q.shape
    tokens, width = residual.shape
    count = len(blocks)

    def kernel(*refs):
        mine, (weight_ref, residual_ref, gain_ref) = refs[: 4 + 2 * count], refs[4 + 2 * count : 7 + 2 * count]
        hidden_ref, *normed_refs = refs[7 + 2 * count : 8 + 2 * count + HALVES]
        held, top, total, acc = refs[-4:]
        attend_body(False, count, [*mine[:4], *block_refs(mine[4:], count), top, total, acc])
        project_body(
            columns, total, acc, weight_ref, residual_ref, gain_ref, hidden_ref, normed_refs, held
        )

    operands = [q, *state] + [a for block in blocks for a in block]
    vmem = pl.BlockSpec(memory_space=pltpu.VMEM)
    return pl.pallas_call(
        kernel,
        out_shape=[
            jax.ShapeDtypeStruct((tokens, width), F32),
        ]
        + [jax.ShapeDtypeStruct((tokens, width // HALVES), BF16)] * HALVES,
        in_specs=[vmem] * (len(operands) + 3),
        out_specs=[vmem] * (1 + HALVES),
        scratch_shapes=[pltpu.VMEM((tokens, width), F32)]
        + [pltpu.VMEM((pairs, rows // 2, lanes), F32)] * 3,
        compiler_params=pltpu.CompilerParams(vmem_limit_bytes=20 * 2**20),
        cost_estimate=cost(1.1 * count + 2),
        name="attend_project",
    )(*operands, out_weight, residual, gain)


def rise_body(parts, blocks, refs):
    pieces = parts * HALVES
    n_refs, gates, ups = refs[:pieces], refs[pieces : pieces + blocks], refs[pieces + blocks : pieces + 2 * blocks]
    act_ref, x_ref = refs[-2:]
    tokens, width = n_refs[0].shape
    for i in range(parts):
        for half in range(HALVES):
            x_ref[i * tokens : (i + 1) * tokens, half * width : (half + 1) * width] = n_refs[i * HALVES + half][...]
    depth, hidden = gates[0].shape
    tile = math.gcd(hidden, 256)

    @pl.loop(0, hidden // tile)
    def _(t):
        cols = pl.ds(pl.multiple_of(t * tile, tile), tile)
        gate = up = None
        for b in range(blocks):
            x = x_ref[:, b * depth : (b + 1) * depth]
            g, u = dot(x, gates[b][:, cols]), dot(x, ups[b][:, cols])
            gate, up = (g, u) if gate is None else (gate + g, up + u)
        act_ref[:, cols] = (gate / (1.0 + jnp.exp(-gate)) * up).astype(BF16)


def rise(normed, gates, ups):
    parts, blocks = len(normed), len(gates)
    tokens, width = normed[0][0].shape
    hidden = gates[0].shape[1]

    def kernel(*refs):
        rise_body(parts, blocks, refs)

    vmem = pl.BlockSpec(memory_space=pltpu.VMEM)
    return pl.pallas_call(
        kernel,
        out_shape=jax.ShapeDtypeStruct((parts * tokens, hidden), BF16),
        in_specs=[vmem] * (parts * HALVES + 2 * blocks),
        out_specs=vmem,
        scratch_shapes=[pltpu.VMEM((parts * tokens, HALVES * width), BF16)],
        compiler_params=pltpu.CompilerParams(vmem_limit_bytes=12 * 2**20),
        cost_estimate=cost(1.5 * parts),
        name="rise",
    )(*[half for chunk in normed for half in chunk], *gates, *ups)


def fall_body(blocks, refs):
    act_ref, downs, outs = refs[0], refs[1 : 1 + blocks], refs[1 + blocks :]
    rows, width = outs[0].shape[0], downs[0].shape[1]
    tile = math.gcd(width, 256)
    for b in range(blocks):

        @pl.loop(0, width // tile)
        def _(t):
            term = dot(act_ref[...], downs[b][:, pl.ds(pl.multiple_of(t * tile, tile), tile)])
            cols = pl.ds(pl.multiple_of(b * width + t * tile, tile), tile)
            for i, out in enumerate(outs):
                out[:, cols] = term[i * rows : (i + 1) * rows].astype(BF16)


def fall(act, parts, downs):
    blocks = len(downs)
    shape = jax.ShapeDtypeStruct((act.shape[0] // parts, blocks * downs[0].shape[1]), BF16)

    def kernel(*refs):
        fall_body(blocks, refs)

    vmem = pl.BlockSpec(memory_space=pltpu.VMEM)
    return pl.pallas_call(
        kernel,
        out_shape=[shape] * parts,
        in_specs=[vmem] * (1 + blocks),
        out_specs=[vmem] * parts,
        compiler_params=pltpu.CompilerParams(vmem_limit_bytes=12 * 2**20),
        cost_estimate=cost(1.2),
        name="fall",
    )(act, *downs)


def finish_body(blocks, hidden_ref, *refs):
    terms, out_ref = refs[:-1], refs[-1]
    each = len(terms) // HALVES
    width = out_ref.shape[1] // blocks
    for b in range(blocks):
        half, column = divmod(b, blocks // HALVES)
        place = pl.ds(pl.multiple_of(block_owner(blocks, b) * width, width), width)
        total = hidden_ref[:, place]
        for term in terms[half * each : (half + 1) * each]:
            total = total + term[:, column * width : (column + 1) * width].astype(F32)
        out_ref[:, place] = total.astype(BF16)


def finish(blocks, hidden_state, terms):
    vmem = pl.BlockSpec(memory_space=pltpu.VMEM)
    operands = [hidden_state] + [term for half in terms for term in half]
    return pl.pallas_call(
        functools.partial(finish_body, blocks),
        out_shape=jax.ShapeDtypeStruct(hidden_state.shape, BF16),
        in_specs=[vmem] * len(operands),
        out_specs=vmem,
        compiler_params=pltpu.CompilerParams(vmem_limit_bytes=8 * 2**20),
        cost_estimate=cost(1),
        name="finish",
    )(*operands)


def tie(array, *others):
    return lax.optimization_barrier((array, *others))[0] if others else array


def shards(
    grps,
    devs,
    residual,
    queries,
    keys,
    values,
    prefix_keys,
    cached_prefix_values,
    out_weight,
    norm_gain,
    w_gate,
    w_up,
    w_down,
    suffix_lengths,
    request_group,
    placement_order,
):
    depth_z = math.gcd(devs, 4)
    depth_y = devs // depth_z
    cores = CORES
    depth_x = grps // cores
    ring = list(range(0, depth_z, 2)) + list(range(1, depth_z, 2))[::-1]

    def shift(by_z, by_y):
        return [
            (
                ring[i] * depth_y + y,
                ring[(i + by_z) % depth_z] * depth_y + (y + by_y) % depth_y,
            )
            for i in range(depth_z)
            for y in range(depth_y)
        ]

    x_shift = [
        (x * cores + c, (x + 1) % depth_x * cores + c) for x in range(depth_x) for c in range(cores)
    ]
    core_swap = [(x * cores + c, x * cores + 1 - c) for x in range(depth_x) for c in range(cores)]

    def round_z(block, *others):
        return lax.ppermute(tie(block, *others), "dev", shift(1, 0))

    def along_y(block, *others):
        return [lax.ppermute(tie(block, *others), "dev", shift(0, ys)) for ys in range(1, depth_y)]

    def along_x(weight, *others):
        blocks = [weight]
        for _ in range(1, depth_x):
            blocks.append(lax.ppermute(tie(blocks[-1], *others), "grp", x_shift))
        return blocks

    def other_core(block, *others):
        return lax.ppermute(tie(block, *others), "grp", core_swap)

    tokens = queries.shape[0]
    width = keys.shape[1]
    groups, span = prefix_keys.shape[:2]

    prefix = jnp.stack([prefix_keys.reshape(-1, width), cached_prefix_values.reshape(-1, width)])
    other = along_y(prefix)
    arriving = round_z(prefix)
    own = jnp.stack([keys, values])
    before = lax.ppermute(own, "dev", [(i, i + 1) for i in range(devs - 1)])
    gate_rows = along_x(w_gate)
    q, before_mask, within_mask, prefix_mask = prepare(
        groups,
        span,
        suffix_lengths,
        request_group,
        placement_order,
        queries,
        width,
    )
    blocks = [(before, before_mask), (own, within_mask), (prefix, prefix_mask)]
    ready, state = [], None
    for zs in range(1, depth_z):
        if zs == depth_z - 1:
            state = attend(q, None, blocks)
            blocks, ready = [], [state[0], gate_swap, *gate_rows[1:]]
        here = tie(arriving, *other, *ready)
        if zs < depth_z - 1:
            arriving, ready = round_z(here), [before]
        blocks += [(b, prefix_mask) for b in other + [here]]
        other = along_y(here)
        if zs == 1:
            gate_swap = other_core(w_gate, here)
        elif zs == 2:
            up_swap = other_core(w_up, here)
    state = attend(q, state, blocks)
    down_swap = other_core(w_down, here)
    up_rows = along_x(w_up, *gate_rows[1:], here)
    gates = [w_gate, gate_swap]
    for gate in gate_rows[1:]:
        gates += [gate, other_core(gate, here)]
    hidden_state, *normed = attend_project(
        q,
        state,
        [(b, prefix_mask) for b in other],
        grps,
        out_weight,
        tie(residual, up_swap, down_swap, *gates[2:]),
        norm_gain[None],
    )

    arrived, across = [normed], [[along_y(half) for half in normed]]
    ups, downs, acts = [w_up, up_swap], [w_down, down_swap], {}
    for zs in range(1, depth_z):
        waits = across[zs - 2] if zs > 1 else [[] for _ in normed]
        arrived.append([round_z(half, *wait) for half, wait in zip(arrived[-1], waits)])
        late = arrived[zs][1:]
        if zs == depth_z - 1:
            acts[1] = rise([arrived[1]] + [list(c) for c in zip(*across[1])], gates, ups)
            late = [*late, acts[1]]
        across.append([along_y(half, *late) for half in arrived[zs]])
        if zs == depth_z - 2:
            for up in up_rows[1:]:
                ups += [up, other_core(up, *arrived[zs], *[b for c in across[zs - 1] for b in c])]
            down_cols = along_x(w_down, *up_rows[1:], *arrived[zs], *[b for c in across[zs - 1] for b in c])
    chunks = [[a] + [list(c) for c in zip(*b)] for a, b in zip(arrived, across)]
    each = grps // HALVES
    acts[2] = rise(chunks[2], gates, ups)
    acts[0] = rise(chunks[0], gates, ups)
    soon = [b for c in across[-1] for b in c] + [acts[2], acts[0]]
    sent = [None] * HALVES
    if each <= len(downs):
        sent[0] = round_z(
            fall(acts[1], 1, downs[:each])[0], *arrived[-1], *[b for c in across[-2] for b in c]
        )
        second = fall(acts[2], 1, downs[:each])[0]
        second = (second.astype(F32) + sent[0].astype(F32)).astype(BF16)
        soon.append(second)
        sent[0] = round_z(second)
    final = depth_z - 1
    for down in down_cols[1:]:
        downs += [down, other_core(down, *soon)]

    terms, fallen = [None] * HALVES, {}
    acts[final] = rise(chunks[final], gates, ups)
    fallen[final, 0] = fall(acts[final], depth_y, downs[:each])
    filler = fallen[final, 0][0]
    for zs in list(range(1, depth_z)) + [0]:
        act = acts[zs]
        for half in range(HALVES):
            joint = sent[half] is not None and sent[half].shape[0] > tokens
            if joint and zs < depth_z - 1:
                continue
            parts = fallen.pop((zs, half), None)
            if parts is None:
                parts = fall(act, depth_y, downs[half * each : (half + 1) * each])
            if joint:
                came = [sent[half][i * tokens : (i + 1) * tokens] for i in range(depth_y)]
                parts = [
                    (part.astype(F32) + share.astype(F32)).astype(BF16) if i else part
                    for i, (part, share) in enumerate(zip(parts, came))
                ]
                terms[half] = [parts[0], came[0]]
            else:
                terms[half] = [parts[0]] + ([round_z(sent[half])] if zs != 1 else [])
            if zs == 0:
                parts = [tie(part, sent[0]) for part in parts]
            terms[half] += [
                lax.ppermute(parts[ys], "dev", shift(0, -ys)) for ys in range(1, depth_y)
            ]
            if zs == 1:
                terms[half][0] = tie(terms[half][0], filler)
            if zs:
                sent[half] = functools.reduce(
                    jnp.add, [term.astype(F32) for term in terms[half]]
                ).astype(BF16)
    return finish(grps, hidden_state, terms)


def solution(mesh):
    placed = (
        P(("grp", "dev"), None),
        P(("grp", "dev"), None),
        P(("grp", "dev"), None),
        P(("grp", "dev"), None),
        P("grp", "dev", None),
        P("grp", "dev", None),
        P(),
        P(),
        P("grp", "dev"),
        P("grp", "dev"),
        P("dev", "grp"),
        P("grp", None),
        P("grp", None),
        P("grp", None),
    )
    return jax.shard_map(
        functools.partial(shards, mesh.shape["grp"], mesh.shape["dev"]),
        mesh=mesh,
        in_specs=placed,
        out_specs=P(("grp", "dev"), None),
        check_vma=False,
    )
```

profile of v0, /device:TPU:0, one launch (start us, length us, event | category | flops | bytes accessed | tf_op | source)
XLA Modules:
  0.0 147.8 jit_solution(13677483649320738266)
XLA Ops:
  1.2 4.1 %collective-permute-start.2 = (bf16[2,256,256]{2,1,0:T(8,128)(2,1)S(1)}, bf16[2,256,256]{2,1,0:T(8,128)(2,1)S(1)}, u32[]{:S(2)}, u32[]{:S(2)}) collective-permute-start(bf16[2,256,256]{2,1,0:T(8,128)(2,1)S(1)} %pad_maximum_fusion.refs_5_), channel_id=1, source_target_pairs={{0,4},{1,5},{4,6},{5,7},{6,2},{7,3},{2,0},{3,1},{8,12},{9,13},{12,... | collective-permute-start | bytes 786440 | tf_op jit(solution)/shard_map/ppermute | solution.py:415
  8.3 2.6 %collective-permute-done.2.refs_9_ = bf16[2,256,256]{2,1,0:T(8,128)(2,1)S(1)} collective-permute-done((bf16[2,256,256]{2,1,0:T(8,128)(2,1)S(1)}, bf16[2,256,256]{2,1,0:T(8,128)(2,1)S(1)}, u32[]{:S(2)}, u32[]{:S(2)}) %collective-permute-start.2) | collective-permute-done | bytes 262176 | tf_op jit(solution)/shard_map/ppermute | solution.py:415
  10.8 2.2 %collective-permute-done.1.refs_7_ = bf16[2,256,256]{2,1,0:T(8,128)(2,1)S(1)} collective-permute-done((bf16[2,256,256]{2,1,0:T(8,128)(2,1)S(1)}, bf16[2,256,256]{2,1,0:T(8,128)(2,1)S(1)}, u32[]{:S(2)}, u32[]{:S(2)}) %collective-permute-start.1) | collective-permute-done | bytes 262176 | tf_op jit(solution)/shard_map/ppermute | solution.py:418
  17.0 2.4 %collective-permute-start = (bf16[2,128,256]{2,1,0:T(8,128)(2,1)S(1)}, bf16[2,128,256]{2,1,0:T(8,128)(2,1)S(1)}, u32[]{:S(2)}, u32[]{:S(2)}) collective-permute-start(bf16[2,128,256]{2,1,0:T(8,128)(2,1)S(1)} %pad_maximum_fusion.1.refs_3_), channel_id=1, source_target_pairs={{0,1},{1,2},{2,3},{3,4},{4,5},{5,6},{6,7},{8,9},{9,10},{10,11},{11... | collective-permute-start | bytes 393224 | tf_op jit(solution)/shard_map/ppermute | solution.py:437
  19.4 5.5 %collective-permute-done.refs_1_ = bf16[2,128,256]{2,1,0:T(8,128)(2,1)S(1)} collective-permute-done((bf16[2,128,256]{2,1,0:T(8,128)(2,1)S(1)}, bf16[2,128,256]{2,1,0:T(8,128)(2,1)S(1)}, u32[]{:S(2)}, u32[]{:S(2)}) %collective-permute-start) | collective-permute-done | bytes 131104 | tf_op jit(solution)/shard_map/ppermute | solution.py:437
  24.9 3.1 %collective-permute-start.6 = (bf16[2,256,256]{2,1,0:T(8,128)(2,1)S(1)}, bf16[2,256,256]{2,1,0:T(8,128)(2,1)S(1)}, u32[]{:S(2)}, u32[]{:S(2)}) collective-permute-start(bf16[2,256,256]{2,1,0:T(8,128)(2,1)S(1)} %collective-permute-done.4.refs_13_), channel_id=1, source_target_pairs={{0,4},{1,5},{4,6},{5,7},{6,2},{7,3},{2,0},{3,1},{8,12},{9,13},{12,... | collective-permute-start | bytes 786440 | tf_op jit(solution)/shard_map/ppermute | solution.py:415
  31.3 4.3 %attend.2 = (f32[2,512,128]{2,1,0:T(8,128)S(1)}, f32[2,512,128]{2,1,0:T(8,128)S(1)}, f32[2,512,128]{2,1,0:T(8,128)S(1)}) custom-call(bf16[2,1024,128]{2,1,0:T(8,128)(2,1)S(1)} %get-tuple-element.56.refs_0_, bf16[2,128,256]{2,1,0:T(8,128)(2,1)S(1)} %collective-permute-done.refs_1_, f32[128,128]{1,0:T(8,128)S(1)} %get-tuple-element.57.refs_2_, ...), custom_call_target="tpu_custom_call" | custom-call | bytes 26950000 | tf_op jit(solution)/shard_map/attend/pallas_call | solution.py:189
  39.8 2.5 %attend.3 = (f32[2,512,128]{2,1,0:T(8,128)S(1)}, f32[2,512,128]{2,1,0:T(8,128)S(1)}, f32[2,512,128]{2,1,0:T(8,128)S(1)}) custom-call(bf16[2,1024,128]{2,1,0:T(8,128)(2,1)S(1)} %get-tuple-element.56.refs_0_, f32[2,512,128]{2,1,0:T(8,128)S(1)} %get-tuple-element.62.refs_1_, f32[2,512,128]{2,1,0:T(8,128)S(1)} %get-tuple-element.63.refs_2_, ...), custom_call_target="tpu_custom_call" | custom-call | bytes 7700000 | tf_op jit(solution)/shard_map/attend/pallas_call | solution.py:189
  42.4 4.0 %collective-permute-done.9.refs_4_ = bf16[2,256,256]{2,1,0:T(8,128)(2,1)S(1)} collective-permute-done((bf16[2,256,256]{2,1,0:T(8,128)(2,1)S(1)}, bf16[2,256,256]{2,1,0:T(8,128)(2,1)S(1)}, u32[]{:S(2)}, u32[]{:S(2)}) %collective-permute-start.9) | collective-permute-done | bytes 262176 | tf_op jit(solution)/shard_map/ppermute | solution.py:418
  46.4 2.4 %attend_project.1 = (f32[128,2048]{1,0:T(8,128)S(1)}, bf16[128,1024]{1,0:T(8,128)(2,1)S(1)}, bf16[128,1024]{1,0:T(8,128)(2,1)S(1)}) custom-call(bf16[2,1024,128]{2,1,0:T(8,128)(2,1)S(1)} %get-tuple-element.56.refs_0_, f32[2,512,128]{2,1,0:T(8,128)S(1)} %get-tuple-element.67.refs_1_, f32[2,512,128]{2,1,0:T(8,128)S(1)} %get-tuple-element.68.refs_2_, ...), custom_call_target="tpu_custom_call" | custom-call | bytes 10850000 | tf_op jit(solution)/shard_map/attend_project/pallas_call | solution.py:252
  50.7 2.0 %collective-permute-start.18 = (bf16[128,1024]{1,0:T(8,128)(2,1)S(1)}, bf16[128,1024]{1,0:T(8,128)(2,1)S(1)}, u32[]{:S(2)}, u32[]{:S(2)}) collective-permute-start(bf16[128,1024]{1,0:T(8,128)(2,1)S(1)} %get-tuple-element.76.refs_1_), channel_id=1, source_target_pairs={{0,4},{1,5},{4,6},{5,7},{6,2},{7,3},{2,0},{3,1},{8,12},{9,13},{12,... | collective-permute-start | bytes 786440 | tf_op jit(solution)/shard_map/ppermute | solution.py:415
  53.4 4.7 %collective-permute-done.16.refs_0_ = bf16[128,1024]{1,0:T(8,128)(2,1)S(1)} collective-permute-done((bf16[128,1024]{1,0:T(8,128)(2,1)S(1)}, bf16[128,1024]{1,0:T(8,128)(2,1)S(1)}, u32[]{:S(2)}, u32[]{:S(2)}) %collective-permute-start.16) | collective-permute-done | bytes 262176 | tf_op jit(solution)/shard_map/ppermute | solution.py:415
  60.6 3.1 %collective-permute-done.18.refs_1_ = bf16[128,1024]{1,0:T(8,128)(2,1)S(1)} collective-permute-done((bf16[128,1024]{1,0:T(8,128)(2,1)S(1)}, bf16[128,1024]{1,0:T(8,128)(2,1)S(1)}, u32[]{:S(2)}, u32[]{:S(2)}) %collective-permute-start.18) | collective-permute-done | bytes 262176 | tf_op jit(solution)/shard_map/ppermute | solution.py:415
  69.4 2.4 %collective-permute-done.20.refs_2_ = bf16[128,1024]{1,0:T(8,128)(2,1)S(1)} collective-permute-done((bf16[128,1024]{1,0:T(8,128)(2,1)S(1)}, bf16[128,1024]{1,0:T(8,128)(2,1)S(1)}, u32[]{:S(2)}, u32[]{:S(2)}) %collective-permute-start.20) | collective-permute-done | bytes 262176 | tf_op jit(solution)/shard_map/ppermute | solution.py:418
  71.7 2.8 %collective-permute-done.21.refs_3_ = bf16[128,1024]{1,0:T(8,128)(2,1)S(1)} collective-permute-done((bf16[128,1024]{1,0:T(8,128)(2,1)S(1)}, bf16[128,1024]{1,0:T(8,128)(2,1)S(1)}, u32[]{:S(2)}, u32[]{:S(2)}) %collective-permute-start.21) | collective-permute-done | bytes 262176 | tf_op jit(solution)/shard_map/ppermute | solution.py:418
  79.7 3.1 %rise.5.refs_0_ = bf16[256,1024]{1,0:T(8,128)(2,1)S(1)} custom-call(bf16[128,1024]{1,0:T(8,128)(2,1)S(1)} %collective-permute-done.16.refs_0_, bf16[128,1024]{1,0:T(8,128)(2,1)S(1)} %collective-permute-done.18.refs_1_, bf16[128,1024]{1,0:T(8,128)(2,1)S(1)} %collective-permute-done.20.refs_2_, bf16[128,1024]{1,0:T(8,128)(2,1)S(1)} %collective-permute-done.21.refs_3_, ...), custom_call_target="tpu_custom_call" | custom-call | bytes 10500000 | tf_op jit(solution)/shard_map/rise/pallas_call | solution.py:299
  84.0 4.9 %collective-permute-done.24.refs_1_ = bf16[128,1024]{1,0:T(8,128)(2,1)S(1)} collective-permute-done((bf16[128,1024]{1,0:T(8,128)(2,1)S(1)}, bf16[128,1024]{1,0:T(8,128)(2,1)S(1)}, u32[]{:S(2)}, u32[]{:S(2)}) %collective-permute-start.24) | collective-permute-done | bytes 262176 | tf_op jit(solution)/shard_map/ppermute | solution.py:415
  90.8 2.2 %collective-permute-start.29 = (bf16[256,1024]{1,0:T(8,128)(2,1)S(1)}, bf16[256,1024]{1,0:T(8,128)(2,1)S(1)}, u32[]{:S(2)}, u32[]{:S(2)}) collective-permute-start(bf16[256,1024]{1,0:T(8,128)(2,1)S(1)} %fall.11), channel_id=1, source_target_pairs={{0,4},{1,5},{4,6},{5,7},{6,2},{7,3},{2,0},{3,1},{8,12},{9,13},{12,... | collective-permute-start | bytes 1572872 | tf_op jit(solution)/shard_map/ppermute | solution.py:415
  95.1 3.1 %rise.4.refs_0_ = bf16[256,1024]{1,0:T(8,128)(2,1)S(1)} custom-call(bf16[128,1024]{1,0:T(8,128)(2,1)S(1)} %get-tuple-element.75.refs_0_, bf16[128,1024]{1,0:T(8,128)(2,1)S(1)} %get-tuple-element.76.refs_1_, bf16[128,1024]{1,0:T(8,128)(2,1)S(1)} %collective-permute-done.13.refs_2_, bf16[128,1024]{1,0:T(8,128)(2,1)S(1)} %collective-permute-done.14.refs_3_, ...), custom_call_target="tpu_custom_call" | custom-call | bytes 10500000 | tf_op jit(solution)/shard_map/rise/pallas_call | solution.py:299
  98.1 3.1 %rise.7.refs_0_ = bf16[256,1024]{1,0:T(8,128)(2,1)S(1)} custom-call(bf16[128,1024]{1,0:T(8,128)(2,1)S(1)} %collective-permute-done.17.refs_0_, bf16[128,1024]{1,0:T(8,128)(2,1)S(1)} %collective-permute-done.19.refs_1_, bf16[128,1024]{1,0:T(8,128)(2,1)S(1)} %collective-permute-done.27.refs_2_, bf16[128,1024]{1,0:T(8,128)(2,1)S(1)} %collective-permute-done.28.refs_3_, ...), custom_call_target="tpu_custom_call" | custom-call | bytes 10500000 | tf_op jit(solution)/shard_map/rise/pallas_call | solution.py:299
  110.6 3.1 %rise.6.refs_0_ = bf16[256,1024]{1,0:T(8,128)(2,1)S(1)} custom-call(bf16[128,1024]{1,0:T(8,128)(2,1)S(1)} %collective-permute-done.23.refs_0_, bf16[128,1024]{1,0:T(8,128)(2,1)S(1)} %collective-permute-done.24.refs_1_, bf16[128,1024]{1,0:T(8,128)(2,1)S(1)} %collective-permute-done.25.refs_2_, bf16[128,1024]{1,0:T(8,128)(2,1)S(1)} %collective-permute-done.26.refs_3_, ...), custom_call_target="tpu_custom_call" | custom-call | bytes 10500000 | tf_op jit(solution)/shard_map/rise/pallas_call | solution.py:299
  125.8 2.4 %collective-permute-start.39 = (bf16[128,1024]{1,0:T(8,128)(2,1)S(1)}, bf16[128,1024]{1,0:T(8,128)(2,1)S(1)}, u32[]{:S(2)}, u32[]{:S(2)}) collective-permute-start(bf16[128,1024]{1,0:T(8,128)(2,1)S(1)} %add_convert_fusion.2), channel_id=1, source_target_pairs={{0,4},{1,5},{4,6},{5,7},{6,2},{7,3},{2,0},{3,1},{8,12},{9,13},{12,... | collective-permute-start | bytes 786440 | tf_op jit(solution)/shard_map/ppermute | solution.py:415
  138.1 4.2 %collective-permute-done.33.refs_2_ = bf16[128,1024]{1,0:T(8,128)(2,1)S(1)} collective-permute-done((bf16[128,1024]{1,0:T(8,128)(2,1)S(1)}, bf16[128,1024]{1,0:T(8,128)(2,1)S(1)}, u32[]{:S(2)}, u32[]{:S(2)}) %collective-permute-start.33) | collective-permute-done | bytes 262176 | tf_op jit(solution)/shard_map/ppermute | solution.py:536
  142.3 4.5 %collective-permute-done.42.refs_5_ = bf16[128,1024]{1,0:T(8,128)(2,1)S(1)} collective-permute-done((bf16[128,1024]{1,0:T(8,128)(2,1)S(1)}, bf16[128,1024]{1,0:T(8,128)(2,1)S(1)}, u32[]{:S(2)}, u32[]{:S(2)}) %collective-permute-start.42) | collective-permute-done | bytes 262176 | tf_op jit(solution)/shard_map/ppermute | solution.py:536
  (102 shorter events, 68.9 us)
Async XLA Ops:
  6.8 29.2 %collective-permute-start.8 = (bf16[512,1024]{1,0:T(8,128)(2,1)}, bf16[512,1024]{1,0:T(8,128)(2,1)S(1)}, u32[]{:S(2)}, u32[]{:S(2)}) collective-permute-start(bf16[512,1024]{1,0:T(8,128)(2,1)} %refs_4_.7), channel_id=1, source_target_pairs={{0,16},{8,24},{16,0},{24,8},{1,17},{9,25},{17,1},{25,9},{2,18},{10... | collective-permute-start | bytes 3145736 | tf_op jit(solution)/shard_map/ppermute | solution.py:423
  13.0 22.9 %collective-permute-start.7 = (bf16[512,1024]{1,0:T(8,128)(2,1)}, bf16[512,1024]{1,0:T(8,128)(2,1)S(1)}, u32[]{:S(2)}, u32[]{:S(2)}) collective-permute-start(bf16[512,1024]{1,0:T(8,128)(2,1)} %refs_4_.7), channel_id=1, source_target_pairs={{0,8},{8,0},{16,24},{24,16},{1,9},{9,1},{17,25},{25,17},{2,10},{10... | collective-permute-start | bytes 3145736 | tf_op jit(solution)/shard_map/ppermute | solution.py:427
  13.0 11.9 %collective-permute-start.4 = (bf16[2,256,256]{2,1,0:T(8,128)(2,1)S(1)}, bf16[2,256,256]{2,1,0:T(8,128)(2,1)S(1)}, u32[]{:S(2)}, u32[]{:S(2)}) collective-permute-start(bf16[2,256,256]{2,1,0:T(8,128)(2,1)S(1)} %collective-permute-done.2.refs_9_), channel_id=1, source_target_pairs={{0,4},{1,5},{4,6},{5,7},{6,2},{7,3},{2,0},{3,1},{8,12},{9,13},{12,... | collective-permute-start | bytes 786440 | tf_op jit(solution)/shard_map/ppermute | solution.py:415
  14.6 10.3 %collective-permute-start.3 = (bf16[2,256,256]{2,1,0:T(8,128)(2,1)S(1)}, bf16[2,256,256]{2,1,0:T(8,128)(2,1)S(1)}, u32[]{:S(2)}, u32[]{:S(2)}) collective-permute-start(bf16[2,256,256]{2,1,0:T(8,128)(2,1)S(1)} %collective-permute-done.2.refs_9_), channel_id=1, source_target_pairs={{0,1},{1,0},{4,5},{5,4},{6,7},{7,6},{2,3},{3,2},{8,9},{9,8},{12,13... | collective-permute-start | bytes 786440 | tf_op jit(solution)/shard_map/ppermute | solution.py:418
  24.9 10.7 %collective-permute-start.6 = (bf16[2,256,256]{2,1,0:T(8,128)(2,1)S(1)}, bf16[2,256,256]{2,1,0:T(8,128)(2,1)S(1)}, u32[]{:S(2)}, u32[]{:S(2)}) collective-permute-start(bf16[2,256,256]{2,1,0:T(8,128)(2,1)S(1)} %collective-permute-done.4.refs_13_), channel_id=1, source_target_pairs={{0,4},{1,5},{4,6},{5,7},{6,2},{7,3},{2,0},{3,1},{8,12},{9,13},{12,... | collective-permute-start | bytes 786440 | tf_op jit(solution)/shard_map/ppermute | solution.py:415
  31.2 11.2 %collective-permute-start.10 = (bf16[512,1024]{1,0:T(8,128)(2,1)}, bf16[512,1024]{1,0:T(8,128)(2,1)S(1)}, u32[]{:S(2)}, u32[]{:S(2)}) collective-permute-start(bf16[512,1024]{1,0:T(8,128)(2,1)} %refs_8_.7), channel_id=1, source_target_pairs={{0,8},{8,0},{16,24},{24,16},{1,9},{9,1},{17,25},{25,17},{2,10},{10... | collective-permute-start | bytes 3145736 | tf_op jit(solution)/shard_map/ppermute | solution.py:427
  36.4 31.0 %collective-permute-start.15 = (bf16[512,1024]{1,0:T(8,128)(2,1)}, bf16[512,1024]{1,0:T(8,128)(2,1)S(1)}, u32[]{:S(2)}, u32[]{:S(2)}) collective-permute-start(bf16[512,1024]{1,0:T(8,128)(2,1)} %refs_8_.7), channel_id=1, source_target_pairs={{0,16},{8,24},{16,0},{24,8},{1,17},{9,25},{17,1},{25,9},{2,18},{10... | collective-permute-start | bytes 3145736 | tf_op jit(solution)/shard_map/ppermute | solution.py:423
  50.7 13.0 %collective-permute-start.18 = (bf16[128,1024]{1,0:T(8,128)(2,1)S(1)}, bf16[128,1024]{1,0:T(8,128)(2,1)S(1)}, u32[]{:S(2)}, u32[]{:S(2)}) collective-permute-start(bf16[128,1024]{1,0:T(8,128)(2,1)S(1)} %get-tuple-element.76.refs_1_), channel_id=1, source_target_pairs={{0,4},{1,5},{4,6},{5,7},{6,2},{7,3},{2,0},{3,1},{8,12},{9,13},{12,... | collective-permute-start | bytes 786440 | tf_op jit(solution)/shard_map/ppermute | solution.py:415
  52.7 13.1 %collective-permute-start.14 = (bf16[128,1024]{1,0:T(8,128)(2,1)S(1)}, bf16[128,1024]{1,0:T(8,128)(2,1)S(1)}, u32[]{:S(2)}, u32[]{:S(2)}) collective-permute-start(bf16[128,1024]{1,0:T(8,128)(2,1)S(1)} %get-tuple-element.76.refs_1_), channel_id=1, source_target_pairs={{0,1},{1,0},{4,5},{5,4},{6,7},{7,6},{2,3},{3,2},{8,9},{9,8},{12,13... | collective-permute-start | bytes 786440 | tf_op jit(solution)/shard_map/ppermute | solution.py:418
  58.9 10.5 %collective-permute-start.17 = (bf16[128,1024]{1,0:T(8,128)(2,1)S(1)}, bf16[128,1024]{1,0:T(8,128)(2,1)S(1)}, u32[]{:S(2)}, u32[]{:S(2)}) collective-permute-start(bf16[128,1024]{1,0:T(8,128)(2,1)S(1)} %collective-permute-done.16.refs_0_), channel_id=1, source_target_pairs={{0,4},{1,5},{4,6},{5,7},{6,2},{7,3},{2,0},{3,1},{8,12},{9,13},{12,... | collective-permute-start | bytes 786440 | tf_op jit(solution)/shard_map/ppermute | solution.py:415
  75.7 13.2 %collective-permute-start.24 = (bf16[128,1024]{1,0:T(8,128)(2,1)S(1)}, bf16[128,1024]{1,0:T(8,128)(2,1)S(1)}, u32[]{:S(2)}, u32[]{:S(2)}) collective-permute-start(bf16[128,1024]{1,0:T(8,128)(2,1)S(1)} %collective-permute-done.19.refs_1_), channel_id=1, source_target_pairs={{0,4},{1,5},{4,6},{5,7},{6,2},{7,3},{2,0},{3,1},{8,12},{9,13},{12,... | collective-permute-start | bytes 786440 | tf_op jit(solution)/shard_map/ppermute | solution.py:415
  77.1 11.9 %collective-permute-start.27 = (bf16[128,1024]{1,0:T(8,128)(2,1)S(1)}, bf16[128,1024]{1,0:T(8,128)(2,1)S(1)}, u32[]{:S(2)}, u32[]{:S(2)}) collective-permute-start(bf16[128,1024]{1,0:T(8,128)(2,1)S(1)} %collective-permute-done.17.refs_0_), channel_id=1, source_target_pairs={{0,1},{1,0},{4,5},{5,4},{6,7},{7,6},{2,3},{3,2},{8,9},{9,8},{12,13... | collective-permute-start | bytes 786440 | tf_op jit(solution)/shard_map/ppermute | solution.py:418
  78.1 12.7 %collective-permute-start.28 = (bf16[128,1024]{1,0:T(8,128)(2,1)S(1)}, bf16[128,1024]{1,0:T(8,128)(2,1)S(1)}, u32[]{:S(2)}, u32[]{:S(2)}) collective-permute-start(bf16[128,1024]{1,0:T(8,128)(2,1)S(1)} %collective-permute-done.19.refs_1_), channel_id=1, source_target_pairs={{0,1},{1,0},{4,5},{5,4},{6,7},{7,6},{2,3},{3,2},{8,9},{9,8},{12,13... | collective-permute-start | bytes 786440 | tf_op jit(solution)/shard_map/ppermute | solution.py:418
  79.1 24.9 %collective-permute-start.34 = (bf16[1024,512]{1,0:T(8,128)(2,1)S(1)}, bf16[1024,512]{1,0:T(8,128)(2,1)S(1)}, u32[]{:S(2)}, u32[]{:S(2)}) collective-permute-start(bf16[1024,512]{1,0:T(8,128)(2,1)S(1)} %copy-done.2), channel_id=1, source_target_pairs={{0,16},{8,24},{16,0},{24,8},{1,17},{9,25},{17,1},{25,9},{2,18},{10... | collective-permute-start | bytes 3145736 | tf_op jit(solution)/shard_map/ppermute | solution.py:423
  90.8 12.9 %collective-permute-start.29 = (bf16[256,1024]{1,0:T(8,128)(2,1)S(1)}, bf16[256,1024]{1,0:T(8,128)(2,1)S(1)}, u32[]{:S(2)}, u32[]{:S(2)}) collective-permute-start(bf16[256,1024]{1,0:T(8,128)(2,1)S(1)} %fall.11), channel_id=1, source_target_pairs={{0,4},{1,5},{4,6},{5,7},{6,2},{7,3},{2,0},{3,1},{8,12},{9,13},{12,... | collective-permute-start | bytes 1572872 | tf_op jit(solution)/shard_map/ppermute | solution.py:415
  93.0 10.9 %collective-permute-start.25 = (bf16[128,1024]{1,0:T(8,128)(2,1)S(1)}, bf16[128,1024]{1,0:T(8,128)(2,1)S(1)}, u32[]{:S(2)}, u32[]{:S(2)}) collective-permute-start(bf16[128,1024]{1,0:T(8,128)(2,1)S(1)} %collective-permute-done.23.refs_0_), channel_id=1, source_target_pairs={{0,1},{1,0},{4,5},{5,4},{6,7},{7,6},{2,3},{3,2},{8,9},{9,8},{12,13... | collective-permute-start | bytes 786440 | tf_op jit(solution)/shard_map/ppermute | solution.py:418
  94.0 11.7 %collective-permute-start.26 = (bf16[128,1024]{1,0:T(8,128)(2,1)S(1)}, bf16[128,1024]{1,0:T(8,128)(2,1)S(1)}, u32[]{:S(2)}, u32[]{:S(2)}) collective-permute-start(bf16[128,1024]{1,0:T(8,128)(2,1)S(1)} %collective-permute-done.24.refs_1_), channel_id=1, source_target_pairs={{0,1},{1,0},{4,5},{5,4},{6,7},{7,6},{2,3},{3,2},{8,9},{9,8},{12,13... | collective-permute-start | bytes 786440 | tf_op jit(solution)/shard_map/ppermute | solution.py:418
  105.7 14.3 %collective-permute-start.30 = (bf16[256,1024]{1,0:T(8,128)(2,1)S(1)}, bf16[256,1024]{1,0:T(8,128)(2,1)S(1)}, u32[]{:S(2)}, u32[]{:S(2)}) collective-permute-start(bf16[256,1024]{1,0:T(8,128)(2,1)S(1)} %add_convert_fusion), channel_id=1, source_target_pairs={{0,4},{1,5},{4,6},{5,7},{6,2},{7,3},{2,0},{3,1},{8,12},{9,13},{12,... | collective-permute-start | bytes 1572872 | tf_op jit(solution)/shard_map/ppermute | solution.py:415
  120.1 10.9 %collective-permute-start.31 = (bf16[128,1024]{1,0:T(8,128)(2,1)S(1)}, bf16[128,1024]{1,0:T(8,128)(2,1)S(1)}, u32[]{:S(2)}, u32[]{:S(2)}) collective-permute-start(bf16[128,1024]{1,0:T(8,128)(2,1)S(1)} %add_convert_fusion.5), channel_id=1, source_target_pairs={{0,1},{1,0},{4,5},{5,4},{6,7},{7,6},{2,3},{3,2},{8,9},{9,8},{12,13... | collective-permute-start | bytes 786440 | tf_op jit(solution)/shard_map/ppermute | solution.py:536
  122.3 14.3 %collective-permute-start.40 = (bf16[128,1024]{1,0:T(8,128)(2,1)S(1)}, bf16[128,1024]{1,0:T(8,128)(2,1)S(1)}, u32[]{:S(2)}, u32[]{:S(2)}) collective-permute-start(bf16[128,1024]{1,0:T(8,128)(2,1)S(1)} %get-tuple-element.104), channel_id=1, source_target_pairs={{0,1},{1,0},{4,5},{5,4},{6,7},{7,6},{2,3},{3,2},{8,9},{9,8},{12,13... | collective-permute-start | bytes 786440 | tf_op jit(solution)/shard_map/ppermute | solution.py:536
  125.8 10.9 %collective-permute-start.39 = (bf16[128,1024]{1,0:T(8,128)(2,1)S(1)}, bf16[128,1024]{1,0:T(8,128)(2,1)S(1)}, u32[]{:S(2)}, u32[]{:S(2)}) collective-permute-start(bf16[128,1024]{1,0:T(8,128)(2,1)S(1)} %add_convert_fusion.2), channel_id=1, source_target_pairs={{0,4},{1,5},{4,6},{5,7},{6,2},{7,3},{2,0},{3,1},{8,12},{9,13},{12,... | collective-permute-start | bytes 786440 | tf_op jit(solution)/shard_map/ppermute | solution.py:415
  131.1 11.1 %collective-permute-start.32 = (bf16[128,1024]{1,0:T(8,128)(2,1)S(1)}, bf16[128,1024]{1,0:T(8,128)(2,1)S(1)}, u32[]{:S(2)}, u32[]{:S(2)}) collective-permute-start(bf16[128,1024]{1,0:T(8,128)(2,1)S(1)} %add_convert_fusion.4), channel_id=1, source_target_pairs={{0,4},{1,5},{4,6},{5,7},{6,2},{7,3},{2,0},{3,1},{8,12},{9,13},{12,... | collective-permute-start | bytes 786440 | tf_op jit(solution)/shard_map/ppermute | solution.py:415
  134.8 11.9 %collective-permute-start.42 = (bf16[128,1024]{1,0:T(8,128)(2,1)S(1)}, bf16[128,1024]{1,0:T(8,128)(2,1)S(1)}, u32[]{:S(2)}, u32[]{:S(2)}) collective-permute-start(bf16[128,1024]{1,0:T(8,128)(2,1)S(1)} %get-tuple-element.106), channel_id=1, source_target_pairs={{0,1},{1,0},{4,5},{5,4},{6,7},{7,6},{2,3},{3,2},{8,9},{9,8},{12,13... | collective-permute-start | bytes 786440 | tf_op jit(solution)/shard_map/ppermute | solution.py:536
  136.8 10.0 %collective-permute-start.41 = (bf16[128,1024]{1,0:T(8,128)(2,1)S(1)}, bf16[128,1024]{1,0:T(8,128)(2,1)S(1)}, u32[]{:S(2)}, u32[]{:S(2)}) collective-permute-start(bf16[128,1024]{1,0:T(8,128)(2,1)S(1)} %add_convert_fusion.1), channel_id=1, source_target_pairs={{0,4},{1,5},{4,6},{5,7},{6,2},{7,3},{2,0},{3,1},{8,12},{9,13},{12,... | collective-permute-start | bytes 786440 | tf_op jit(solution)/shard_map/ppermute | solution.py:415
  (26 other events, 372.4 us)
where the time goes:
time: 148 us
  waiting for transfers between devices  55.7 us (38%)
  starting transfers between devices  53.4 us (36%)
  Pallas kernels  34 us (23%)
  other arithmetic  3.41 us (2%)
    ppermute x15, starting transfers between devices, round_z(): return lax.ppermute(tie(block, *others), 'dev', shift(1, 0))  27.8 us
    ppermute x15, waiting for transfers between devices, round_z(): return lax.ppermute(tie(block, *others), 'dev', shift(1, 0))  19.3 us
    ppermute x12, waiting for transfers between devices, along_y(): lax.ppermute(tie(block, *others), 'dev', shift(0, ys))  16.1 us
    ppermute x6, waiting for transfers between devices, shards(): lax.ppermute(parts[ys], 'dev', shift(0, -ys))  13.8 us
    ppermute x12, starting transfers between devices, along_y(): lax.ppermute(tie(block, *others), 'dev', shift(0, ys))  12.7 us
    pallas_call x4, Pallas kernels, rise(): pl.pallas_call(kernel, out_shape=jax.ShapeDtypeStruct((parts * tokens, hi...  12.3 us
    pallas_call x8, Pallas kernels, fall(): pl.pallas_call(kernel, out_shape=[shape] * parts, in_specs=[vmem] * (1 +...  9.81 us
    pallas_call x2, Pallas kernels, attend(): pl.pallas_call(kernel, out_shape=[shape] * 3, in_specs=[vmem] * len(opera...  6.85 us
  transfers between devices with their start and end apart: 43, of which 24 were waited for; matrix products, arithmetic and copies ran while one was open for 2% of the time, Pallas kernels for 22%

commit v1 on v0

--- a/solution.py
+++ b/solution.py
@@ -446,14 +446,14 @@
         width,
     )
     blocks = [(before, before_mask), (own, within_mask), (prefix, prefix_mask)]
-    ready, state = [], None
+    ready, state = [before], None
     for zs in range(1, depth_z):
         if zs == depth_z - 1:
             state = attend(q, None, blocks)
             blocks, ready = [], [state[0], gate_swap, *gate_rows[1:]]
         here = tie(arriving, *other, *ready)
         if zs < depth_z - 1:
-            arriving, ready = round_z(here), [before]
+            arriving, ready = round_z(here), [q]
         blocks += [(b, prefix_mask) for b in other + [here]]
         other = along_y(here)
         if zs == 1:

time: 148 us -> 146 us (0.986)
  starting transfers between devices: 53.4 us -> 51.1 us
    ppermute x1, waiting for transfers between devices: 5.45 us -> 3.22 us  [shards(): before = lax.ppermute(own, 'dev', [(i, i + 1) for i in range(devs - 1)])]
    ppermute x15, starting transfers between devices: 27.8 us -> 25.6 us  [round_z(): return lax.ppermute(tie(block, *others), 'dev', shift(1, 0))]
  transfers between devices with their start and end apart: 43 -> 43, of which waited for: 24 -> 24; matrix products, arithmetic and copies ran while one was open for 2% -> 2% of each run, Pallas kernels for 22% -> 23%
where the time goes in v1:
time: 146 us
  waiting for transfers between devices  55.9 us (38%)
  starting transfers between devices  51.1 us (35%)
  Pallas kernels  34 us (23%)
  other arithmetic  3.41 us (2%)
    ppermute x15, starting transfers between devices, round_z(): return lax.ppermute(tie(block, *others), 'dev', shift(1, 0))  25.6 us
    ppermute x15, waiting for transfers between devices, round_z(): return lax.ppermute(tie(block, *others), 'dev', shift(1, 0))  20.6 us
    ppermute x12, waiting for transfers between devices, along_y(): lax.ppermute(tie(block, *others), 'dev', shift(0, ys))  16.5 us
    ppermute x6, waiting for transfers between devices, shards(): lax.ppermute(parts[ys], 'dev', shift(0, -ys))  14.5 us
    ppermute x12, starting transfers between devices, along_y(): lax.ppermute(tie(block, *others), 'dev', shift(0, ys))  12.7 us
    pallas_call x4, Pallas kernels, rise(): pl.pallas_call(kernel, out_shape=jax.ShapeDtypeStruct((parts * tokens, hi...  12.3 us
    pallas_call x8, Pallas kernels, fall(): pl.pallas_call(kernel, out_shape=[shape] * parts, in_specs=[vmem] * (1 +...  9.81 us
    pallas_call x2, Pallas kernels, attend(): pl.pallas_call(kernel, out_shape=[shape] * 3, in_specs=[vmem] * len(opera...  6.84 us
  transfers between devices with their start and end apart: 43, of which 24 were waited for; matrix products, arithmetic and copies ran while one was open for 2% of the time, Pallas kernels for 23%

profile of v1, /device:TPU:0, one launch (start us, length us, event | category | flops | bytes accessed | tf_op | source)
XLA Modules:
  0.0 145.8 jit_solution(1953112831353317514)
XLA Ops:
  1.2 4.1 %collective-permute-start.2 = (bf16[2,256,256]{2,1,0:T(8,128)(2,1)S(1)}, bf16[2,256,256]{2,1,0:T(8,128)(2,1)S(1)}, u32[]{:S(2)}, u32[]{:S(2)}) collective-permute-start(bf16[2,256,256]{2,1,0:T(8,128)(2,1)S(1)} %pad_maximum_fusion.refs_5_), channel_id=1, source_target_pairs={{0,4},{1,5},{4,6},{5,7},{6,2},{7,3},{2,0},{3,1},{8,12},{9,13},{12,... | collective-permute-start | bytes 786440 | tf_op jit(solution)/shard_map/ppermute | solution.py:415
  7.6 2.4 %collective-permute-start = (bf16[2,128,256]{2,1,0:T(8,128)(2,1)S(1)}, bf16[2,128,256]{2,1,0:T(8,128)(2,1)S(1)}, u32[]{:S(2)}, u32[]{:S(2)}) collective-permute-start(bf16[2,128,256]{2,1,0:T(8,128)(2,1)S(1)} %pad_maximum_fusion.1.refs_3_), channel_id=1, source_target_pairs={{0,1},{1,2},{2,3},{3,4},{4,5},{5,6},{6,7},{8,9},{9,10},{10,11},{11... | collective-permute-start | bytes 393224 | tf_op jit(solution)/shard_map/ppermute | solution.py:437
  11.6 3.2 %collective-permute-done.refs_1_ = bf16[2,128,256]{2,1,0:T(8,128)(2,1)S(1)} collective-permute-done((bf16[2,128,256]{2,1,0:T(8,128)(2,1)S(1)}, bf16[2,128,256]{2,1,0:T(8,128)(2,1)S(1)}, u32[]{:S(2)}, u32[]{:S(2)}) %collective-permute-start) | collective-permute-done | bytes 131104 | tf_op jit(solution)/shard_map/ppermute | solution.py:437
  14.9 3.2 %collective-permute-start.4 = (bf16[2,256,256]{2,1,0:T(8,128)(2,1)S(1)}, bf16[2,256,256]{2,1,0:T(8,128)(2,1)S(1)}, u32[]{:S(2)}, u32[]{:S(2)}) collective-permute-start(bf16[2,256,256]{2,1,0:T(8,128)(2,1)S(1)} %collective-permute-done.2.refs_9_), channel_id=1, source_target_pairs={{0,4},{1,5},{4,6},{5,7},{6,2},{7,3},{2,0},{3,1},{8,12},{9,13},{12,... | collective-permute-start | bytes 786440 | tf_op jit(solution)/shard_map/ppermute | solution.py:415
  22.2 2.0 %collective-permute-done.4.refs_13_ = bf16[2,256,256]{2,1,0:T(8,128)(2,1)S(1)} collective-permute-done((bf16[2,256,256]{2,1,0:T(8,128)(2,1)S(1)}, bf16[2,256,256]{2,1,0:T(8,128)(2,1)S(1)}, u32[]{:S(2)}, u32[]{:S(2)}) %collective-permute-start.4) | collective-permute-done | bytes 262176 | tf_op jit(solution)/shard_map/ppermute | solution.py:415
  24.2 2.2 %collective-permute-done.3.refs_11_ = bf16[2,256,256]{2,1,0:T(8,128)(2,1)S(1)} collective-permute-done((bf16[2,256,256]{2,1,0:T(8,128)(2,1)S(1)}, bf16[2,256,256]{2,1,0:T(8,128)(2,1)S(1)}, u32[]{:S(2)}, u32[]{:S(2)}) %collective-permute-start.3) | collective-permute-done | bytes 262176 | tf_op jit(solution)/shard_map/ppermute | solution.py:418
  28.5 4.3 %attend.2 = (f32[2,512,128]{2,1,0:T(8,128)S(1)}, f32[2,512,128]{2,1,0:T(8,128)S(1)}, f32[2,512,128]{2,1,0:T(8,128)S(1)}) custom-call(bf16[2,1024,128]{2,1,0:T(8,128)(2,1)S(1)} %get-tuple-element.56.refs_0_, bf16[2,128,256]{2,1,0:T(8,128)(2,1)S(1)} %collective-permute-done.refs_1_, f32[128,128]{1,0:T(8,128)S(1)} %get-tuple-element.57.refs_2_, ...), custom_call_target="tpu_custom_call" | custom-call | bytes 26950000 | tf_op jit(solution)/shard_map/attend/pallas_call | solution.py:189
  38.2 2.5 %attend.3 = (f32[2,512,128]{2,1,0:T(8,128)S(1)}, f32[2,512,128]{2,1,0:T(8,128)S(1)}, f32[2,512,128]{2,1,0:T(8,128)S(1)}) custom-call(bf16[2,1024,128]{2,1,0:T(8,128)(2,1)S(1)} %get-tuple-element.56.refs_0_, f32[2,512,128]{2,1,0:T(8,128)S(1)} %get-tuple-element.62.refs_1_, f32[2,512,128]{2,1,0:T(8,128)S(1)} %get-tuple-element.63.refs_2_, ...), custom_call_target="tpu_custom_call" | custom-call | bytes 7700000 | tf_op jit(solution)/shard_map/attend/pallas_call | solution.py:189
  40.8 4.4 %collective-permute-done.9.refs_4_ = bf16[2,256,256]{2,1,0:T(8,128)(2,1)S(1)} collective-permute-done((bf16[2,256,256]{2,1,0:T(8,128)(2,1)S(1)}, bf16[2,256,256]{2,1,0:T(8,128)(2,1)S(1)}, u32[]{:S(2)}, u32[]{:S(2)}) %collective-permute-start.9) | collective-permute-done | bytes 262176 | tf_op jit(solution)/shard_map/ppermute | solution.py:418
  45.2 2.4 %attend_project.1 = (f32[128,2048]{1,0:T(8,128)S(1)}, bf16[128,1024]{1,0:T(8,128)(2,1)S(1)}, bf16[128,1024]{1,0:T(8,128)(2,1)S(1)}) custom-call(bf16[2,1024,128]{2,1,0:T(8,128)(2,1)S(1)} %get-tuple-element.56.refs_0_, f32[2,512,128]{2,1,0:T(8,128)S(1)} %get-tuple-element.67.refs_1_, f32[2,512,128]{2,1,0:T(8,128)S(1)} %get-tuple-element.68.refs_2_, ...), custom_call_target="tpu_custom_call" | custom-call | bytes 10850000 | tf_op jit(solution)/shard_map/attend_project/pallas_call | solution.py:252
  51.7 5.2 %collective-permute-done.16.refs_0_ = bf16[128,1024]{1,0:T(8,128)(2,1)S(1)} collective-permute-done((bf16[128,1024]{1,0:T(8,128)(2,1)S(1)}, bf16[128,1024]{1,0:T(8,128)(2,1)S(1)}, u32[]{:S(2)}, u32[]{:S(2)}) %collective-permute-start.16) | collective-permute-done | bytes 262176 | tf_op jit(solution)/shard_map/ppermute | solution.py:415
  59.1 3.5 %collective-permute-done.18.refs_1_ = bf16[128,1024]{1,0:T(8,128)(2,1)S(1)} collective-permute-done((bf16[128,1024]{1,0:T(8,128)(2,1)S(1)}, bf16[128,1024]{1,0:T(8,128)(2,1)S(1)}, u32[]{:S(2)}, u32[]{:S(2)}) %collective-permute-start.18) | collective-permute-done | bytes 262176 | tf_op jit(solution)/shard_map/ppermute | solution.py:415
  64.6 2.2 %collective-permute-start.19 = (bf16[128,1024]{1,0:T(8,128)(2,1)S(1)}, bf16[128,1024]{1,0:T(8,128)(2,1)S(1)}, u32[]{:S(2)}, u32[]{:S(2)}) collective-permute-start(bf16[128,1024]{1,0:T(8,128)(2,1)S(1)} %collective-permute-done.18.refs_1_), channel_id=1, source_target_pairs={{0,4},{1,5},{4,6},{5,7},{6,2},{7,3},{2,0},{3,1},{8,12},{9,13},{12,... | collective-permute-start | bytes 786440 | tf_op jit(solution)/shard_map/ppermute | solution.py:415
  69.8 2.8 %collective-permute-done.21.refs_3_ = bf16[128,1024]{1,0:T(8,128)(2,1)S(1)} collective-permute-done((bf16[128,1024]{1,0:T(8,128)(2,1)S(1)}, bf16[128,1024]{1,0:T(8,128)(2,1)S(1)}, u32[]{:S(2)}, u32[]{:S(2)}) %collective-permute-start.21) | collective-permute-done | bytes 262176 | tf_op jit(solution)/shard_map/ppermute | solution.py:418
  77.4 3.1 %rise.5.refs_0_ = bf16[256,1024]{1,0:T(8,128)(2,1)S(1)} custom-call(bf16[128,1024]{1,0:T(8,128)(2,1)S(1)} %collective-permute-done.16.refs_0_, bf16[128,1024]{1,0:T(8,128)(2,1)S(1)} %collective-permute-done.18.refs_1_, bf16[128,1024]{1,0:T(8,128)(2,1)S(1)} %collective-permute-done.20.refs_2_, bf16[128,1024]{1,0:T(8,128)(2,1)S(1)} %collective-permute-done.21.refs_3_, ...), custom_call_target="tpu_custom_call" | custom-call | bytes 10500000 | tf_op jit(solution)/shard_map/rise/pallas_call | solution.py:299
  81.7 5.2 %collective-permute-done.24.refs_1_ = bf16[128,1024]{1,0:T(8,128)(2,1)S(1)} collective-permute-done((bf16[128,1024]{1,0:T(8,128)(2,1)S(1)}, bf16[128,1024]{1,0:T(8,128)(2,1)S(1)}, u32[]{:S(2)}, u32[]{:S(2)}) %collective-permute-start.24) | collective-permute-done | bytes 262176 | tf_op jit(solution)/shard_map/ppermute | solution.py:415
  92.4 3.1 %rise.4.refs_0_ = bf16[256,1024]{1,0:T(8,128)(2,1)S(1)} custom-call(bf16[128,1024]{1,0:T(8,128)(2,1)S(1)} %get-tuple-element.75.refs_0_, bf16[128,1024]{1,0:T(8,128)(2,1)S(1)} %get-tuple-element.76.refs_1_, bf16[128,1024]{1,0:T(8,128)(2,1)S(1)} %collective-permute-done.13.refs_2_, bf16[128,1024]{1,0:T(8,128)(2,1)S(1)} %collective-permute-done.14.refs_3_, ...), custom_call_target="tpu_custom_call" | custom-call | bytes 10500000 | tf_op jit(solution)/shard_map/rise/pallas_call | solution.py:299
  95.5 3.1 %rise.7.refs_0_ = bf16[256,1024]{1,0:T(8,128)(2,1)S(1)} custom-call(bf16[128,1024]{1,0:T(8,128)(2,1)S(1)} %collective-permute-done.17.refs_0_, bf16[128,1024]{1,0:T(8,128)(2,1)S(1)} %collective-permute-done.19.refs_1_, bf16[128,1024]{1,0:T(8,128)(2,1)S(1)} %collective-permute-done.27.refs_2_, bf16[128,1024]{1,0:T(8,128)(2,1)S(1)} %collective-permute-done.28.refs_3_, ...), custom_call_target="tpu_custom_call" | custom-call | bytes 10500000 | tf_op jit(solution)/shard_map/rise/pallas_call | solution.py:299
  108.5 3.1 %rise.6.refs_0_ = bf16[256,1024]{1,0:T(8,128)(2,1)S(1)} custom-call(bf16[128,1024]{1,0:T(8,128)(2,1)S(1)} %collective-permute-done.23.refs_0_, bf16[128,1024]{1,0:T(8,128)(2,1)S(1)} %collective-permute-done.24.refs_1_, bf16[128,1024]{1,0:T(8,128)(2,1)S(1)} %collective-permute-done.25.refs_2_, bf16[128,1024]{1,0:T(8,128)(2,1)S(1)} %collective-permute-done.26.refs_3_, ...), custom_call_target="tpu_custom_call" | custom-call | bytes 10500000 | tf_op jit(solution)/shard_map/rise/pallas_call | solution.py:299
  120.8 2.5 %collective-permute-done.38 = bf16[128,1024]{1,0:T(8,128)(2,1)S(1)} collective-permute-done((bf16[128,1024]{1,0:T(8,128)(2,1)S(1)}, bf16[128,1024]{1,0:T(8,128)(2,1)S(1)}, u32[]{:S(2)}, u32[]{:S(2)}) %collective-permute-start.38) | collective-permute-done | bytes 262176 | tf_op jit(solution)/shard_map/ppermute | solution.py:536
  123.5 2.1 %collective-permute-start.39 = (bf16[128,1024]{1,0:T(8,128)(2,1)S(1)}, bf16[128,1024]{1,0:T(8,128)(2,1)S(1)}, u32[]{:S(2)}, u32[]{:S(2)}) collective-permute-start(bf16[128,1024]{1,0:T(8,128)(2,1)S(1)} %add_convert_fusion.2), channel_id=1, source_target_pairs={{0,4},{1,5},{4,6},{5,7},{6,2},{7,3},{2,0},{3,1},{8,12},{9,13},{12,... | collective-permute-start | bytes 786440 | tf_op jit(solution)/shard_map/ppermute | solution.py:415
  126.7 2.2 %collective-permute-done.31 = bf16[128,1024]{1,0:T(8,128)(2,1)S(1)} collective-permute-done((bf16[128,1024]{1,0:T(8,128)(2,1)S(1)}, bf16[128,1024]{1,0:T(8,128)(2,1)S(1)}, u32[]{:S(2)}, u32[]{:S(2)}) %collective-permute-start.31) | collective-permute-done | bytes 262176 | tf_op jit(solution)/shard_map/ppermute | solution.py:536
  136.2 3.9 %collective-permute-done.33.refs_2_ = bf16[128,1024]{1,0:T(8,128)(2,1)S(1)} collective-permute-done((bf16[128,1024]{1,0:T(8,128)(2,1)S(1)}, bf16[128,1024]{1,0:T(8,128)(2,1)S(1)}, u32[]{:S(2)}, u32[]{:S(2)}) %collective-permute-start.33) | collective-permute-done | bytes 262176 | tf_op jit(solution)/shard_map/ppermute | solution.py:536
  140.2 4.5 %collective-permute-done.42.refs_5_ = bf16[128,1024]{1,0:T(8,128)(2,1)S(1)} collective-permute-done((bf16[128,1024]{1,0:T(8,128)(2,1)S(1)}, bf16[128,1024]{1,0:T(8,128)(2,1)S(1)}, u32[]{:S(2)}, u32[]{:S(2)}) %collective-permute-start.42) | collective-permute-done | bytes 262176 | tf_op jit(solution)/shard_map/ppermute | solution.py:536
  (102 shorter events, 68.4 us)
Async XLA Ops:
  1.2 13.7 %collective-permute-start.2 = (bf16[2,256,256]{2,1,0:T(8,128)(2,1)S(1)}, bf16[2,256,256]{2,1,0:T(8,128)(2,1)S(1)}, u32[]{:S(2)}, u32[]{:S(2)}) collective-permute-start(bf16[2,256,256]{2,1,0:T(8,128)(2,1)S(1)} %pad_maximum_fusion.refs_5_), channel_id=1, source_target_pairs={{0,4},{1,5},{4,6},{5,7},{6,2},{7,3},{2,0},{3,1},{8,12},{9,13},{12,... | collective-permute-start | bytes 786440 | tf_op jit(solution)/shard_map/ppermute | solution.py:415
  5.2 9.6 %collective-permute-start.1 = (bf16[2,256,256]{2,1,0:T(8,128)(2,1)S(1)}, bf16[2,256,256]{2,1,0:T(8,128)(2,1)S(1)}, u32[]{:S(2)}, u32[]{:S(2)}) collective-permute-start(bf16[2,256,256]{2,1,0:T(8,128)(2,1)S(1)} %pad_maximum_fusion.refs_5_), channel_id=1, source_target_pairs={{0,1},{1,0},{4,5},{5,4},{6,7},{7,6},{2,3},{3,2},{8,9},{9,8},{12,13... | collective-permute-start | bytes 786440 | tf_op jit(solution)/shard_map/ppermute | solution.py:418
  10.1 25.1 %collective-permute-start.8 = (bf16[512,1024]{1,0:T(8,128)(2,1)}, bf16[512,1024]{1,0:T(8,128)(2,1)S(1)}, u32[]{:S(2)}, u32[]{:S(2)}) collective-permute-start(bf16[512,1024]{1,0:T(8,128)(2,1)} %refs_4_.7), channel_id=1, source_target_pairs={{0,16},{8,24},{16,0},{24,8},{1,17},{9,25},{17,1},{25,9},{2,18},{10... | collective-permute-start | bytes 3145736 | tf_op jit(solution)/shard_map/ppermute | solution.py:423
  14.9 20.3 %collective-permute-start.7 = (bf16[512,1024]{1,0:T(8,128)(2,1)}, bf16[512,1024]{1,0:T(8,128)(2,1)S(1)}, u32[]{:S(2)}, u32[]{:S(2)}) collective-permute-start(bf16[512,1024]{1,0:T(8,128)(2,1)} %refs_4_.7), channel_id=1, source_target_pairs={{0,8},{8,0},{16,24},{24,16},{1,9},{9,1},{17,25},{25,17},{2,10},{10... | collective-permute-start | bytes 3145736 | tf_op jit(solution)/shard_map/ppermute | solution.py:427
  28.5 12.2 %collective-permute-start.10 = (bf16[512,1024]{1,0:T(8,128)(2,1)}, bf16[512,1024]{1,0:T(8,128)(2,1)S(1)}, u32[]{:S(2)}, u32[]{:S(2)}) collective-permute-start(bf16[512,1024]{1,0:T(8,128)(2,1)} %refs_8_.7), channel_id=1, source_target_pairs={{0,8},{8,0},{16,24},{24,16},{1,9},{9,1},{17,25},{25,17},{2,10},{10... | collective-permute-start | bytes 3145736 | tf_op jit(solution)/shard_map/ppermute | solution.py:427
  35.7 31.0 %collective-permute-start.15 = (bf16[512,1024]{1,0:T(8,128)(2,1)}, bf16[512,1024]{1,0:T(8,128)(2,1)S(1)}, u32[]{:S(2)}, u32[]{:S(2)}) collective-permute-start(bf16[512,1024]{1,0:T(8,128)(2,1)} %refs_8_.7), channel_id=1, source_target_pairs={{0,16},{8,24},{16,0},{24,8},{1,17},{9,25},{17,1},{25,9},{2,18},{10... | collective-permute-start | bytes 3145736 | tf_op jit(solution)/shard_map/ppermute | solution.py:423
  49.9 12.6 %collective-permute-start.18 = (bf16[128,1024]{1,0:T(8,128)(2,1)S(1)}, bf16[128,1024]{1,0:T(8,128)(2,1)S(1)}, u32[]{:S(2)}, u32[]{:S(2)}) collective-permute-start(bf16[128,1024]{1,0:T(8,128)(2,1)S(1)} %get-tuple-element.76.refs_1_), channel_id=1, source_target_pairs={{0,4},{1,5},{4,6},{5,7},{6,2},{7,3},{2,0},{3,1},{8,12},{9,13},{12,... | collective-permute-start | bytes 786440 | tf_op jit(solution)/shard_map/ppermute | solution.py:415
  50.5 14.1 %collective-permute-start.14 = (bf16[128,1024]{1,0:T(8,128)(2,1)S(1)}, bf16[128,1024]{1,0:T(8,128)(2,1)S(1)}, u32[]{:S(2)}, u32[]{:S(2)}) collective-permute-start(bf16[128,1024]{1,0:T(8,128)(2,1)S(1)} %get-tuple-element.76.refs_1_), channel_id=1, source_target_pairs={{0,1},{1,0},{4,5},{5,4},{6,7},{7,6},{2,3},{3,2},{8,9},{9,8},{12,13... | collective-permute-start | bytes 786440 | tf_op jit(solution)/shard_map/ppermute | solution.py:418
  58.2 10.0 %collective-permute-start.17 = (bf16[128,1024]{1,0:T(8,128)(2,1)S(1)}, bf16[128,1024]{1,0:T(8,128)(2,1)S(1)}, u32[]{:S(2)}, u32[]{:S(2)}) collective-permute-start(bf16[128,1024]{1,0:T(8,128)(2,1)S(1)} %collective-permute-done.16.refs_0_), channel_id=1, source_target_pairs={{0,4},{1,5},{4,6},{5,7},{6,2},{7,3},{2,0},{3,1},{8,12},{9,13},{12,... | collective-permute-start | bytes 786440 | tf_op jit(solution)/shard_map/ppermute | solution.py:415
  74.4 12.6 %collective-permute-start.24 = (bf16[128,1024]{1,0:T(8,128)(2,1)S(1)}, bf16[128,1024]{1,0:T(8,128)(2,1)S(1)}, u32[]{:S(2)}, u32[]{:S(2)}) collective-permute-start(bf16[128,1024]{1,0:T(8,128)(2,1)S(1)} %collective-permute-done.19.refs_1_), channel_id=1, source_target_pairs={{0,4},{1,5},{4,6},{5,7},{6,2},{7,3},{2,0},{3,1},{8,12},{9,13},{12,... | collective-permute-start | bytes 786440 | tf_op jit(solution)/shard_map/ppermute | solution.py:415
  74.8 12.1 %collective-permute-start.27 = (bf16[128,1024]{1,0:T(8,128)(2,1)S(1)}, bf16[128,1024]{1,0:T(8,128)(2,1)S(1)}, u32[]{:S(2)}, u32[]{:S(2)}) collective-permute-start(bf16[128,1024]{1,0:T(8,128)(2,1)S(1)} %collective-permute-done.17.refs_0_), channel_id=1, source_target_pairs={{0,1},{1,0},{4,5},{5,4},{6,7},{7,6},{2,3},{3,2},{8,9},{9,8},{12,13... | collective-permute-start | bytes 786440 | tf_op jit(solution)/shard_map/ppermute | solution.py:418
  76.5 12.1 %collective-permute-start.28 = (bf16[128,1024]{1,0:T(8,128)(2,1)S(1)}, bf16[128,1024]{1,0:T(8,128)(2,1)S(1)}, u32[]{:S(2)}, u32[]{:S(2)}) collective-permute-start(bf16[128,1024]{1,0:T(8,128)(2,1)S(1)} %collective-permute-done.19.refs_1_), channel_id=1, source_target_pairs={{0,1},{1,0},{4,5},{5,4},{6,7},{7,6},{2,3},{3,2},{8,9},{9,8},{12,13... | collective-permute-start | bytes 786440 | tf_op jit(solution)/shard_map/ppermute | solution.py:418
  76.9 24.9 %collective-permute-start.34 = (bf16[1024,512]{1,0:T(8,128)(2,1)S(1)}, bf16[1024,512]{1,0:T(8,128)(2,1)S(1)}, u32[]{:S(2)}, u32[]{:S(2)}) collective-permute-start(bf16[1024,512]{1,0:T(8,128)(2,1)S(1)} %copy-done.2), channel_id=1, source_target_pairs={{0,16},{8,24},{16,0},{24,8},{1,17},{9,25},{17,1},{25,9},{2,18},{10... | collective-permute-start | bytes 3145736 | tf_op jit(solution)/shard_map/ppermute | solution.py:423
  88.6 12.9 %collective-permute-start.29 = (bf16[256,1024]{1,0:T(8,128)(2,1)S(1)}, bf16[256,1024]{1,0:T(8,128)(2,1)S(1)}, u32[]{:S(2)}, u32[]{:S(2)}) collective-permute-start(bf16[256,1024]{1,0:T(8,128)(2,1)S(1)} %fall.11), channel_id=1, source_target_pairs={{0,4},{1,5},{4,6},{5,7},{6,2},{7,3},{2,0},{3,1},{8,12},{9,13},{12,... | collective-permute-start | bytes 1572872 | tf_op jit(solution)/shard_map/ppermute | solution.py:415
  90.4 11.4 %collective-permute-start.25 = (bf16[128,1024]{1,0:T(8,128)(2,1)S(1)}, bf16[128,1024]{1,0:T(8,128)(2,1)S(1)}, u32[]{:S(2)}, u32[]{:S(2)}) collective-permute-start(bf16[128,1024]{1,0:T(8,128)(2,1)S(1)} %collective-permute-done.23.refs_0_), channel_id=1, source_target_pairs={{0,1},{1,0},{4,5},{5,4},{6,7},{7,6},{2,3},{3,2},{8,9},{9,8},{12,13... | collective-permute-start | bytes 786440 | tf_op jit(solution)/shard_map/ppermute | solution.py:418
  91.9 11.1 %collective-permute-start.26 = (bf16[128,1024]{1,0:T(8,128)(2,1)S(1)}, bf16[128,1024]{1,0:T(8,128)(2,1)S(1)}, u32[]{:S(2)}, u32[]{:S(2)}) collective-permute-start(bf16[128,1024]{1,0:T(8,128)(2,1)S(1)} %collective-permute-done.24.refs_1_), channel_id=1, source_target_pairs={{0,1},{1,0},{4,5},{5,4},{6,7},{7,6},{2,3},{3,2},{8,9},{9,8},{12,13... | collective-permute-start | bytes 786440 | tf_op jit(solution)/shard_map/ppermute | solution.py:418
  103.0 14.3 %collective-permute-start.30 = (bf16[256,1024]{1,0:T(8,128)(2,1)S(1)}, bf16[256,1024]{1,0:T(8,128)(2,1)S(1)}, u32[]{:S(2)}, u32[]{:S(2)}) collective-permute-start(bf16[256,1024]{1,0:T(8,128)(2,1)S(1)} %add_convert_fusion), channel_id=1, source_target_pairs={{0,4},{1,5},{4,6},{5,7},{6,2},{7,3},{2,0},{3,1},{8,12},{9,13},{12,... | collective-permute-start | bytes 1572872 | tf_op jit(solution)/shard_map/ppermute | solution.py:415
  117.4 11.5 %collective-permute-start.31 = (bf16[128,1024]{1,0:T(8,128)(2,1)S(1)}, bf16[128,1024]{1,0:T(8,128)(2,1)S(1)}, u32[]{:S(2)}, u32[]{:S(2)}) collective-permute-start(bf16[128,1024]{1,0:T(8,128)(2,1)S(1)} %add_convert_fusion.5), channel_id=1, source_target_pairs={{0,1},{1,0},{4,5},{5,4},{6,7},{7,6},{2,3},{3,2},{8,9},{9,8},{12,13... | collective-permute-start | bytes 786440 | tf_op jit(solution)/shard_map/ppermute | solution.py:536
  120.3 14.3 %collective-permute-start.40 = (bf16[128,1024]{1,0:T(8,128)(2,1)S(1)}, bf16[128,1024]{1,0:T(8,128)(2,1)S(1)}, u32[]{:S(2)}, u32[]{:S(2)}) collective-permute-start(bf16[128,1024]{1,0:T(8,128)(2,1)S(1)} %get-tuple-element.104), channel_id=1, source_target_pairs={{0,1},{1,0},{4,5},{5,4},{6,7},{7,6},{2,3},{3,2},{8,9},{9,8},{12,13... | collective-permute-start | bytes 786440 | tf_op jit(solution)/shard_map/ppermute | solution.py:536
  123.5 11.1 %collective-permute-start.39 = (bf16[128,1024]{1,0:T(8,128)(2,1)S(1)}, bf16[128,1024]{1,0:T(8,128)(2,1)S(1)}, u32[]{:S(2)}, u32[]{:S(2)}) collective-permute-start(bf16[128,1024]{1,0:T(8,128)(2,1)S(1)} %add_convert_fusion.2), channel_id=1, source_target_pairs={{0,4},{1,5},{4,6},{5,7},{6,2},{7,3},{2,0},{3,1},{8,12},{9,13},{12,... | collective-permute-start | bytes 786440 | tf_op jit(solution)/shard_map/ppermute | solution.py:415
  129.1 11.1 %collective-permute-start.32 = (bf16[128,1024]{1,0:T(8,128)(2,1)S(1)}, bf16[128,1024]{1,0:T(8,128)(2,1)S(1)}, u32[]{:S(2)}, u32[]{:S(2)}) collective-permute-start(bf16[128,1024]{1,0:T(8,128)(2,1)S(1)} %add_convert_fusion.4), channel_id=1, source_target_pairs={{0,4},{1,5},{4,6},{5,7},{6,2},{7,3},{2,0},{3,1},{8,12},{9,13},{12,... | collective-permute-start | bytes 786440 | tf_op jit(solution)/shard_map/ppermute | solution.py:415
  130.6 9.6 %collective-permute-start.33 = (bf16[128,1024]{1,0:T(8,128)(2,1)S(1)}, bf16[128,1024]{1,0:T(8,128)(2,1)S(1)}, u32[]{:S(2)}, u32[]{:S(2)}) collective-permute-start(bf16[128,1024]{1,0:T(8,128)(2,1)S(1)} %get-tuple-element.94), channel_id=1, source_target_pairs={{0,1},{1,0},{4,5},{5,4},{6,7},{7,6},{2,3},{3,2},{8,9},{9,8},{12,13... | collective-permute-start | bytes 786440 | tf_op jit(solution)/shard_map/ppermute | solution.py:536
  132.1 12.6 %collective-permute-start.42 = (bf16[128,1024]{1,0:T(8,128)(2,1)S(1)}, bf16[128,1024]{1,0:T(8,128)(2,1)S(1)}, u32[]{:S(2)}, u32[]{:S(2)}) collective-permute-start(bf16[128,1024]{1,0:T(8,128)(2,1)S(1)} %get-tuple-element.106), channel_id=1, source_target_pairs={{0,1},{1,0},{4,5},{5,4},{6,7},{7,6},{2,3},{3,2},{8,9},{9,8},{12,13... | collective-permute-start | bytes 786440 | tf_op jit(solution)/shard_map/ppermute | solution.py:536
  134.7 10.0 %collective-permute-start.41 = (bf16[128,1024]{1,0:T(8,128)(2,1)S(1)}, bf16[128,1024]{1,0:T(8,128)(2,1)S(1)}, u32[]{:S(2)}, u32[]{:S(2)}) collective-permute-start(bf16[128,1024]{1,0:T(8,128)(2,1)S(1)} %add_convert_fusion.1), channel_id=1, source_target_pairs={{0,4},{1,5},{4,6},{5,7},{6,2},{7,3},{2,0},{3,1},{8,12},{9,13},{12,... | collective-permute-start | bytes 786440 | tf_op jit(solution)/shard_map/ppermute | solution.py:415
  (26 other events, 369.3 us)

commit v2 on v1

--- a/solution.py
+++ b/solution.py
@@ -451,7 +451,7 @@
         if zs == depth_z - 1:
             state = attend(q, None, blocks)
             blocks, ready = [], [state[0], gate_swap, *gate_rows[1:]]
-        here = tie(arriving, *other, *ready)
+        here = tie(arriving, *(other if zs != 2 else []), *ready)
         if zs < depth_z - 1:
             arriving, ready = round_z(here), [q]
         blocks += [(b, prefix_mask) for b in other + [here]]

time: 146 us -> 146 us (level)
  starting transfers between devices: 51.1 us -> 54 us
  waiting for transfers between devices: 55.9 us -> 53 us
    ppermute x15, starting transfers between devices: 25.6 us -> 27.9 us  [round_z(): return lax.ppermute(tie(block, *others), 'dev', shift(1, 0))]
  transfers between devices with their start and end apart: 43 -> 43, of which waited for: 24 -> 23; matrix products, arithmetic and copies ran while one was open for 2% -> 2% of each run, Pallas kernels for 23% -> 23%
where the time goes in v2:
time: 146 us
  starting transfers between devices  54 us (37%)
  waiting for transfers between devices  53 us (36%)
  Pallas kernels  34 us (23%)
  other arithmetic  3.41 us (2%)
    ppermute x15, starting transfers between devices, round_z(): return lax.ppermute(tie(block, *others), 'dev', shift(1, 0))  27.9 us
    ppermute x15, waiting for transfers between devices, round_z(): return lax.ppermute(tie(block, *others), 'dev', shift(1, 0))  19.2 us
    ppermute x12, waiting for transfers between devices, along_y(): lax.ppermute(tie(block, *others), 'dev', shift(0, ys))  15.6 us
    ppermute x6, waiting for transfers between devices, shards(): lax.ppermute(parts[ys], 'dev', shift(0, -ys))  13.8 us
    ppermute x12, starting transfers between devices, along_y(): lax.ppermute(tie(block, *others), 'dev', shift(0, ys))  13.2 us
    pallas_call x4, Pallas kernels, rise(): pl.pallas_call(kernel, out_shape=jax.ShapeDtypeStruct((parts * tokens, hi...  12.3 us
    pallas_call x8, Pallas kernels, fall(): pl.pallas_call(kernel, out_shape=[shape] * parts, in_specs=[vmem] * (1 +...  9.82 us
    pallas_call x2, Pallas kernels, attend(): pl.pallas_call(kernel, out_shape=[shape] * 3, in_specs=[vmem] * len(opera...  6.84 us
  transfers between devices with their start and end apart: 43, of which 23 were waited for; matrix products, arithmetic and copies ran while one was open for 2% of the time, Pallas kernels for 23%

profile of v2, /device:TPU:0, one launch (start us, length us, event | category | flops | bytes accessed | tf_op | source)
XLA Modules:
  0.0 145.7 jit_solution(11744609662235882171)
XLA Ops:
  1.2 4.1 %collective-permute-start.2 = (bf16[2,256,256]{2,1,0:T(8,128)(2,1)S(1)}, bf16[2,256,256]{2,1,0:T(8,128)(2,1)S(1)}, u32[]{:S(2)}, u32[]{:S(2)}) collective-permute-start(bf16[2,256,256]{2,1,0:T(8,128)(2,1)S(1)} %pad_maximum_fusion.refs_5_), channel_id=1, source_target_pairs={{0,4},{1,5},{4,6},{5,7},{6,2},{7,3},{2,0},{3,1},{8,12},{9,13},{12,... | collective-permute-start | bytes 786440 | tf_op jit(solution)/shard_map/ppermute | solution.py:415
  7.6 2.4 %collective-permute-start = (bf16[2,128,256]{2,1,0:T(8,128)(2,1)S(1)}, bf16[2,128,256]{2,1,0:T(8,128)(2,1)S(1)}, u32[]{:S(2)}, u32[]{:S(2)}) collective-permute-start(bf16[2,128,256]{2,1,0:T(8,128)(2,1)S(1)} %pad_maximum_fusion.1.refs_3_), channel_id=1, source_target_pairs={{0,1},{1,2},{2,3},{3,4},{4,5},{5,6},{6,7},{8,9},{9,10},{10,11},{11... | collective-permute-start | bytes 393224 | tf_op jit(solution)/shard_map/ppermute | solution.py:437
  11.6 3.2 %collective-permute-done.refs_1_ = bf16[2,128,256]{2,1,0:T(8,128)(2,1)S(1)} collective-permute-done((bf16[2,128,256]{2,1,0:T(8,128)(2,1)S(1)}, bf16[2,128,256]{2,1,0:T(8,128)(2,1)S(1)}, u32[]{:S(2)}, u32[]{:S(2)}) %collective-permute-start) | collective-permute-done | bytes 131104 | tf_op jit(solution)/shard_map/ppermute | solution.py:437
  14.9 3.2 %collective-permute-start.4 = (bf16[2,256,256]{2,1,0:T(8,128)(2,1)S(1)}, bf16[2,256,256]{2,1,0:T(8,128)(2,1)S(1)}, u32[]{:S(2)}, u32[]{:S(2)}) collective-permute-start(bf16[2,256,256]{2,1,0:T(8,128)(2,1)S(1)} %collective-permute-done.2.refs_9_), channel_id=1, source_target_pairs={{0,4},{1,5},{4,6},{5,7},{6,2},{7,3},{2,0},{3,1},{8,12},{9,13},{12,... | collective-permute-start | bytes 786440 | tf_op jit(solution)/shard_map/ppermute | solution.py:415
  24.2 3.4 %collective-permute-start.6 = (bf16[2,256,256]{2,1,0:T(8,128)(2,1)S(1)}, bf16[2,256,256]{2,1,0:T(8,128)(2,1)S(1)}, u32[]{:S(2)}, u32[]{:S(2)}) collective-permute-start(bf16[2,256,256]{2,1,0:T(8,128)(2,1)S(1)} %collective-permute-done.4.refs_13_), channel_id=1, source_target_pairs={{0,4},{1,5},{4,6},{5,7},{6,2},{7,3},{2,0},{3,1},{8,12},{9,13},{12,... | collective-permute-start | bytes 786440 | tf_op jit(solution)/shard_map/ppermute | solution.py:415
  28.5 4.3 %attend.2 = (f32[2,512,128]{2,1,0:T(8,128)S(1)}, f32[2,512,128]{2,1,0:T(8,128)S(1)}, f32[2,512,128]{2,1,0:T(8,128)S(1)}) custom-call(bf16[2,1024,128]{2,1,0:T(8,128)(2,1)S(1)} %get-tuple-element.56.refs_0_, bf16[2,128,256]{2,1,0:T(8,128)(2,1)S(1)} %collective-permute-done.refs_1_, f32[128,128]{1,0:T(8,128)S(1)} %get-tuple-element.57.refs_2_, ...), custom_call_target="tpu_custom_call" | custom-call | bytes 26950000 | tf_op jit(solution)/shard_map/attend/pallas_call | solution.py:189
  33.0 2.2 %collective-permute-done.5.refs_4_ = bf16[2,256,256]{2,1,0:T(8,128)(2,1)S(1)} collective-permute-done((bf16[2,256,256]{2,1,0:T(8,128)(2,1)S(1)}, bf16[2,256,256]{2,1,0:T(8,128)(2,1)S(1)}, u32[]{:S(2)}, u32[]{:S(2)}) %collective-permute-start.5) | collective-permute-done | bytes 262176 | tf_op jit(solution)/shard_map/ppermute | solution.py:418
  38.1 2.5 %attend.3 = (f32[2,512,128]{2,1,0:T(8,128)S(1)}, f32[2,512,128]{2,1,0:T(8,128)S(1)}, f32[2,512,128]{2,1,0:T(8,128)S(1)}) custom-call(bf16[2,1024,128]{2,1,0:T(8,128)(2,1)S(1)} %get-tuple-element.56.refs_0_, f32[2,512,128]{2,1,0:T(8,128)S(1)} %get-tuple-element.62.refs_1_, f32[2,512,128]{2,1,0:T(8,128)S(1)} %get-tuple-element.63.refs_2_, ...), custom_call_target="tpu_custom_call" | custom-call | bytes 7700000 | tf_op jit(solution)/shard_map/attend/pallas_call | solution.py:189
  40.8 4.4 %collective-permute-done.9.refs_4_ = bf16[2,256,256]{2,1,0:T(8,128)(2,1)S(1)} collective-permute-done((bf16[2,256,256]{2,1,0:T(8,128)(2,1)S(1)}, bf16[2,256,256]{2,1,0:T(8,128)(2,1)S(1)}, u32[]{:S(2)}, u32[]{:S(2)}) %collective-permute-start.9) | collective-permute-done | bytes 262176 | tf_op jit(solution)/shard_map/ppermute | solution.py:418
  45.2 2.4 %attend_project.1 = (f32[128,2048]{1,0:T(8,128)S(1)}, bf16[128,1024]{1,0:T(8,128)(2,1)S(1)}, bf16[128,1024]{1,0:T(8,128)(2,1)S(1)}) custom-call(bf16[2,1024,128]{2,1,0:T(8,128)(2,1)S(1)} %get-tuple-element.56.refs_0_, f32[2,512,128]{2,1,0:T(8,128)S(1)} %get-tuple-element.67.refs_1_, f32[2,512,128]{2,1,0:T(8,128)S(1)} %get-tuple-element.68.refs_2_, ...), custom_call_target="tpu_custom_call" | custom-call | bytes 10850000 | tf_op jit(solution)/shard_map/attend_project/pallas_call | solution.py:252
  51.7 5.2 %collective-permute-done.16.refs_0_ = bf16[128,1024]{1,0:T(8,128)(2,1)S(1)} collective-permute-done((bf16[128,1024]{1,0:T(8,128)(2,1)S(1)}, bf16[128,1024]{1,0:T(8,128)(2,1)S(1)}, u32[]{:S(2)}, u32[]{:S(2)}) %collective-permute-start.16) | collective-permute-done | bytes 262176 | tf_op jit(solution)/shard_map/ppermute | solution.py:415
  59.1 3.5 %collective-permute-done.18.refs_1_ = bf16[128,1024]{1,0:T(8,128)(2,1)S(1)} collective-permute-done((bf16[128,1024]{1,0:T(8,128)(2,1)S(1)}, bf16[128,1024]{1,0:T(8,128)(2,1)S(1)}, u32[]{:S(2)}, u32[]{:S(2)}) %collective-permute-start.18) | collective-permute-done | bytes 262176 | tf_op jit(solution)/shard_map/ppermute | solution.py:415
  64.5 2.2 %collective-permute-start.19 = (bf16[128,1024]{1,0:T(8,128)(2,1)S(1)}, bf16[128,1024]{1,0:T(8,128)(2,1)S(1)}, u32[]{:S(2)}, u32[]{:S(2)}) collective-permute-start(bf16[128,1024]{1,0:T(8,128)(2,1)S(1)} %collective-permute-done.18.refs_1_), channel_id=1, source_target_pairs={{0,4},{1,5},{4,6},{5,7},{6,2},{7,3},{2,0},{3,1},{8,12},{9,13},{12,... | collective-permute-start | bytes 786440 | tf_op jit(solution)/shard_map/ppermute | solution.py:415
  69.8 2.8 %collective-permute-done.21.refs_3_ = bf16[128,1024]{1,0:T(8,128)(2,1)S(1)} collective-permute-done((bf16[128,1024]{1,0:T(8,128)(2,1)S(1)}, bf16[128,1024]{1,0:T(8,128)(2,1)S(1)}, u32[]{:S(2)}, u32[]{:S(2)}) %collective-permute-start.21) | collective-permute-done | bytes 262176 | tf_op jit(solution)/shard_map/ppermute | solution.py:418
  77.6 3.1 %rise.5.refs_0_ = bf16[256,1024]{1,0:T(8,128)(2,1)S(1)} custom-call(bf16[128,1024]{1,0:T(8,128)(2,1)S(1)} %collective-permute-done.16.refs_0_, bf16[128,1024]{1,0:T(8,128)(2,1)S(1)} %collective-permute-done.18.refs_1_, bf16[128,1024]{1,0:T(8,128)(2,1)S(1)} %collective-permute-done.20.refs_2_, bf16[128,1024]{1,0:T(8,128)(2,1)S(1)} %collective-permute-done.21.refs_3_, ...), custom_call_target="tpu_custom_call" | custom-call | bytes 10500000 | tf_op jit(solution)/shard_map/rise/pallas_call | solution.py:299
  81.9 5.1 %collective-permute-done.24.refs_1_ = bf16[128,1024]{1,0:T(8,128)(2,1)S(1)} collective-permute-done((bf16[128,1024]{1,0:T(8,128)(2,1)S(1)}, bf16[128,1024]{1,0:T(8,128)(2,1)S(1)}, u32[]{:S(2)}, u32[]{:S(2)}) %collective-permute-start.24) | collective-permute-done | bytes 262176 | tf_op jit(solution)/shard_map/ppermute | solution.py:415
  88.8 1.9 %collective-permute-start.29 = (bf16[256,1024]{1,0:T(8,128)(2,1)S(1)}, bf16[256,1024]{1,0:T(8,128)(2,1)S(1)}, u32[]{:S(2)}, u32[]{:S(2)}) collective-permute-start(bf16[256,1024]{1,0:T(8,128)(2,1)S(1)} %fall.11), channel_id=1, source_target_pairs={{0,4},{1,5},{4,6},{5,7},{6,2},{7,3},{2,0},{3,1},{8,12},{9,13},{12,... | collective-permute-start | bytes 1572872 | tf_op jit(solution)/shard_map/ppermute | solution.py:415
  92.7 3.1 %rise.4.refs_0_ = bf16[256,1024]{1,0:T(8,128)(2,1)S(1)} custom-call(bf16[128,1024]{1,0:T(8,128)(2,1)S(1)} %get-tuple-element.75.refs_0_, bf16[128,1024]{1,0:T(8,128)(2,1)S(1)} %get-tuple-element.76.refs_1_, bf16[128,1024]{1,0:T(8,128)(2,1)S(1)} %collective-permute-done.13.refs_2_, bf16[128,1024]{1,0:T(8,128)(2,1)S(1)} %collective-permute-done.14.refs_3_, ...), custom_call_target="tpu_custom_call" | custom-call | bytes 10500000 | tf_op jit(solution)/shard_map/rise/pallas_call | solution.py:299
  95.8 3.1 %rise.7.refs_0_ = bf16[256,1024]{1,0:T(8,128)(2,1)S(1)} custom-call(bf16[128,1024]{1,0:T(8,128)(2,1)S(1)} %collective-permute-done.17.refs_0_, bf16[128,1024]{1,0:T(8,128)(2,1)S(1)} %collective-permute-done.19.refs_1_, bf16[128,1024]{1,0:T(8,128)(2,1)S(1)} %collective-permute-done.27.refs_2_, bf16[128,1024]{1,0:T(8,128)(2,1)S(1)} %collective-permute-done.28.refs_3_, ...), custom_call_target="tpu_custom_call" | custom-call | bytes 10500000 | tf_op jit(solution)/shard_map/rise/pallas_call | solution.py:299
  108.5 3.1 %rise.6.refs_0_ = bf16[256,1024]{1,0:T(8,128)(2,1)S(1)} custom-call(bf16[128,1024]{1,0:T(8,128)(2,1)S(1)} %collective-permute-done.23.refs_0_, bf16[128,1024]{1,0:T(8,128)(2,1)S(1)} %collective-permute-done.24.refs_1_, bf16[128,1024]{1,0:T(8,128)(2,1)S(1)} %collective-permute-done.25.refs_2_, bf16[128,1024]{1,0:T(8,128)(2,1)S(1)} %collective-permute-done.26.refs_3_, ...), custom_call_target="tpu_custom_call" | custom-call | bytes 10500000 | tf_op jit(solution)/shard_map/rise/pallas_call | solution.py:299
  121.1 2.2 %collective-permute-done.38 = bf16[128,1024]{1,0:T(8,128)(2,1)S(1)} collective-permute-done((bf16[128,1024]{1,0:T(8,128)(2,1)S(1)}, bf16[128,1024]{1,0:T(8,128)(2,1)S(1)}, u32[]{:S(2)}, u32[]{:S(2)}) %collective-permute-start.38) | collective-permute-done | bytes 262176 | tf_op jit(solution)/shard_map/ppermute | solution.py:536
  123.5 2.4 %collective-permute-start.39 = (bf16[128,1024]{1,0:T(8,128)(2,1)S(1)}, bf16[128,1024]{1,0:T(8,128)(2,1)S(1)}, u32[]{:S(2)}, u32[]{:S(2)}) collective-permute-start(bf16[128,1024]{1,0:T(8,128)(2,1)S(1)} %add_convert_fusion.2), channel_id=1, source_target_pairs={{0,4},{1,5},{4,6},{5,7},{6,2},{7,3},{2,0},{3,1},{8,12},{9,13},{12,... | collective-permute-start | bytes 786440 | tf_op jit(solution)/shard_map/ppermute | solution.py:415
  136.2 4.0 %collective-permute-done.33.refs_2_ = bf16[128,1024]{1,0:T(8,128)(2,1)S(1)} collective-permute-done((bf16[128,1024]{1,0:T(8,128)(2,1)S(1)}, bf16[128,1024]{1,0:T(8,128)(2,1)S(1)}, u32[]{:S(2)}, u32[]{:S(2)}) %collective-permute-start.33) | collective-permute-done | bytes 262176 | tf_op jit(solution)/shard_map/ppermute | solution.py:536
  140.2 4.5 %collective-permute-done.42.refs_5_ = bf16[128,1024]{1,0:T(8,128)(2,1)S(1)} collective-permute-done((bf16[128,1024]{1,0:T(8,128)(2,1)S(1)}, bf16[128,1024]{1,0:T(8,128)(2,1)S(1)}, u32[]{:S(2)}, u32[]{:S(2)}) %collective-permute-start.42) | collective-permute-done | bytes 262176 | tf_op jit(solution)/shard_map/ppermute | solution.py:536
  (102 shorter events, 67.4 us)
Async XLA Ops:
  1.2 13.7 %collective-permute-start.2 = (bf16[2,256,256]{2,1,0:T(8,128)(2,1)S(1)}, bf16[2,256,256]{2,1,0:T(8,128)(2,1)S(1)}, u32[]{:S(2)}, u32[]{:S(2)}) collective-permute-start(bf16[2,256,256]{2,1,0:T(8,128)(2,1)S(1)} %pad_maximum_fusion.refs_5_), channel_id=1, source_target_pairs={{0,4},{1,5},{4,6},{5,7},{6,2},{7,3},{2,0},{3,1},{8,12},{9,13},{12,... | collective-permute-start | bytes 786440 | tf_op jit(solution)/shard_map/ppermute | solution.py:415
  5.2 9.6 %collective-permute-start.1 = (bf16[2,256,256]{2,1,0:T(8,128)(2,1)S(1)}, bf16[2,256,256]{2,1,0:T(8,128)(2,1)S(1)}, u32[]{:S(2)}, u32[]{:S(2)}) collective-permute-start(bf16[2,256,256]{2,1,0:T(8,128)(2,1)S(1)} %pad_maximum_fusion.refs_5_), channel_id=1, source_target_pairs={{0,1},{1,0},{4,5},{5,4},{6,7},{7,6},{2,3},{3,2},{8,9},{9,8},{12,13... | collective-permute-start | bytes 786440 | tf_op jit(solution)/shard_map/ppermute | solution.py:418
  10.1 25.1 %collective-permute-start.8 = (bf16[512,1024]{1,0:T(8,128)(2,1)}, bf16[512,1024]{1,0:T(8,128)(2,1)S(1)}, u32[]{:S(2)}, u32[]{:S(2)}) collective-permute-start(bf16[512,1024]{1,0:T(8,128)(2,1)} %refs_4_.7), channel_id=1, source_target_pairs={{0,16},{8,24},{16,0},{24,8},{1,17},{9,25},{17,1},{25,9},{2,18},{10... | collective-permute-start | bytes 3145736 | tf_op jit(solution)/shard_map/ppermute | solution.py:423
  14.9 20.3 %collective-permute-start.7 = (bf16[512,1024]{1,0:T(8,128)(2,1)}, bf16[512,1024]{1,0:T(8,128)(2,1)S(1)}, u32[]{:S(2)}, u32[]{:S(2)}) collective-permute-start(bf16[512,1024]{1,0:T(8,128)(2,1)} %refs_4_.7), channel_id=1, source_target_pairs={{0,8},{8,0},{16,24},{24,16},{1,9},{9,1},{17,25},{25,17},{2,10},{10... | collective-permute-start | bytes 3145736 | tf_op jit(solution)/shard_map/ppermute | solution.py:427
  18.7 9.8 %collective-permute-start.3 = (bf16[2,256,256]{2,1,0:T(8,128)(2,1)S(1)}, bf16[2,256,256]{2,1,0:T(8,128)(2,1)S(1)}, u32[]{:S(2)}, u32[]{:S(2)}) collective-permute-start(bf16[2,256,256]{2,1,0:T(8,128)(2,1)S(1)} %collective-permute-done.2.refs_9_), channel_id=1, source_target_pairs={{0,1},{1,0},{4,5},{5,4},{6,7},{7,6},{2,3},{3,2},{8,9},{9,8},{12,13... | collective-permute-start | bytes 786440 | tf_op jit(solution)/shard_map/ppermute | solution.py:418
  28.5 12.2 %collective-permute-start.10 = (bf16[512,1024]{1,0:T(8,128)(2,1)}, bf16[512,1024]{1,0:T(8,128)(2,1)S(1)}, u32[]{:S(2)}, u32[]{:S(2)}) collective-permute-start(bf16[512,1024]{1,0:T(8,128)(2,1)} %refs_8_.7), channel_id=1, source_target_pairs={{0,8},{8,0},{16,24},{24,16},{1,9},{9,1},{17,25},{25,17},{2,10},{10... | collective-permute-start | bytes 3145736 | tf_op jit(solution)/shard_map/ppermute | solution.py:427
  35.7 31.0 %collective-permute-start.15 = (bf16[512,1024]{1,0:T(8,128)(2,1)}, bf16[512,1024]{1,0:T(8,128)(2,1)S(1)}, u32[]{:S(2)}, u32[]{:S(2)}) collective-permute-start(bf16[512,1024]{1,0:T(8,128)(2,1)} %refs_8_.7), channel_id=1, source_target_pairs={{0,16},{8,24},{16,0},{24,8},{1,17},{9,25},{17,1},{25,9},{2,18},{10... | collective-permute-start | bytes 3145736 | tf_op jit(solution)/shard_map/ppermute | solution.py:423
  49.9 12.6 %collective-permute-start.18 = (bf16[128,1024]{1,0:T(8,128)(2,1)S(1)}, bf16[128,1024]{1,0:T(8,128)(2,1)S(1)}, u32[]{:S(2)}, u32[]{:S(2)}) collective-permute-start(bf16[128,1024]{1,0:T(8,128)(2,1)S(1)} %get-tuple-element.76.refs_1_), channel_id=1, source_target_pairs={{0,4},{1,5},{4,6},{5,7},{6,2},{7,3},{2,0},{3,1},{8,12},{9,13},{12,... | collective-permute-start | bytes 786440 | tf_op jit(solution)/shard_map/ppermute | solution.py:415
  50.0 14.6 %collective-permute-start.14 = (bf16[128,1024]{1,0:T(8,128)(2,1)S(1)}, bf16[128,1024]{1,0:T(8,128)(2,1)S(1)}, u32[]{:S(2)}, u32[]{:S(2)}) collective-permute-start(bf16[128,1024]{1,0:T(8,128)(2,1)S(1)} %get-tuple-element.76.refs_1_), channel_id=1, source_target_pairs={{0,1},{1,0},{4,5},{5,4},{6,7},{7,6},{2,3},{3,2},{8,9},{9,8},{12,13... | collective-permute-start | bytes 786440 | tf_op jit(solution)/shard_map/ppermute | solution.py:418
  58.2 10.0 %collective-permute-start.17 = (bf16[128,1024]{1,0:T(8,128)(2,1)S(1)}, bf16[128,1024]{1,0:T(8,128)(2,1)S(1)}, u32[]{:S(2)}, u32[]{:S(2)}) collective-permute-start(bf16[128,1024]{1,0:T(8,128)(2,1)S(1)} %collective-permute-done.16.refs_0_), channel_id=1, source_target_pairs={{0,4},{1,5},{4,6},{5,7},{6,2},{7,3},{2,0},{3,1},{8,12},{9,13},{12,... | collective-permute-start | bytes 786440 | tf_op jit(solution)/shard_map/ppermute | solution.py:415
  74.4 12.6 %collective-permute-start.24 = (bf16[128,1024]{1,0:T(8,128)(2,1)S(1)}, bf16[128,1024]{1,0:T(8,128)(2,1)S(1)}, u32[]{:S(2)}, u32[]{:S(2)}) collective-permute-start(bf16[128,1024]{1,0:T(8,128)(2,1)S(1)} %collective-permute-done.19.refs_1_), channel_id=1, source_target_pairs={{0,4},{1,5},{4,6},{5,7},{6,2},{7,3},{2,0},{3,1},{8,12},{9,13},{12,... | collective-permute-start | bytes 786440 | tf_op jit(solution)/shard_map/ppermute | solution.py:415
  75.0 12.0 %collective-permute-start.27 = (bf16[128,1024]{1,0:T(8,128)(2,1)S(1)}, bf16[128,1024]{1,0:T(8,128)(2,1)S(1)}, u32[]{:S(2)}, u32[]{:S(2)}) collective-permute-start(bf16[128,1024]{1,0:T(8,128)(2,1)S(1)} %collective-permute-done.17.refs_0_), channel_id=1, source_target_pairs={{0,1},{1,0},{4,5},{5,4},{6,7},{7,6},{2,3},{3,2},{8,9},{9,8},{12,13... | collective-permute-start | bytes 786440 | tf_op jit(solution)/shard_map/ppermute | solution.py:418
  76.5 12.3 %collective-permute-start.28 = (bf16[128,1024]{1,0:T(8,128)(2,1)S(1)}, bf16[128,1024]{1,0:T(8,128)(2,1)S(1)}, u32[]{:S(2)}, u32[]{:S(2)}) collective-permute-start(bf16[128,1024]{1,0:T(8,128)(2,1)S(1)} %collective-permute-done.19.refs_1_), channel_id=1, source_target_pairs={{0,1},{1,0},{4,5},{5,4},{6,7},{7,6},{2,3},{3,2},{8,9},{9,8},{12,13... | collective-permute-start | bytes 786440 | tf_op jit(solution)/shard_map/ppermute | solution.py:418
  77.0 24.9 %collective-permute-start.34 = (bf16[1024,512]{1,0:T(8,128)(2,1)S(1)}, bf16[1024,512]{1,0:T(8,128)(2,1)S(1)}, u32[]{:S(2)}, u32[]{:S(2)}) collective-permute-start(bf16[1024,512]{1,0:T(8,128)(2,1)S(1)} %copy-done.2), channel_id=1, source_target_pairs={{0,16},{8,24},{16,0},{24,8},{1,17},{9,25},{17,1},{25,9},{2,18},{10... | collective-permute-start | bytes 3145736 | tf_op jit(solution)/shard_map/ppermute | solution.py:423
  88.8 12.9 %collective-permute-start.29 = (bf16[256,1024]{1,0:T(8,128)(2,1)S(1)}, bf16[256,1024]{1,0:T(8,128)(2,1)S(1)}, u32[]{:S(2)}, u32[]{:S(2)}) collective-permute-start(bf16[256,1024]{1,0:T(8,128)(2,1)S(1)} %fall.11), channel_id=1, source_target_pairs={{0,4},{1,5},{4,6},{5,7},{6,2},{7,3},{2,0},{3,1},{8,12},{9,13},{12,... | collective-permute-start | bytes 1572872 | tf_op jit(solution)/shard_map/ppermute | solution.py:415
  90.7 11.2 %collective-permute-start.25 = (bf16[128,1024]{1,0:T(8,128)(2,1)S(1)}, bf16[128,1024]{1,0:T(8,128)(2,1)S(1)}, u32[]{:S(2)}, u32[]{:S(2)}) collective-permute-start(bf16[128,1024]{1,0:T(8,128)(2,1)S(1)} %collective-permute-done.23.refs_0_), channel_id=1, source_target_pairs={{0,1},{1,0},{4,5},{5,4},{6,7},{7,6},{2,3},{3,2},{8,9},{9,8},{12,13... | collective-permute-start | bytes 786440 | tf_op jit(solution)/shard_map/ppermute | solution.py:418
  91.9 11.4 %collective-permute-start.26 = (bf16[128,1024]{1,0:T(8,128)(2,1)S(1)}, bf16[128,1024]{1,0:T(8,128)(2,1)S(1)}, u32[]{:S(2)}, u32[]{:S(2)}) collective-permute-start(bf16[128,1024]{1,0:T(8,128)(2,1)S(1)} %collective-permute-done.24.refs_1_), channel_id=1, source_target_pairs={{0,1},{1,0},{4,5},{5,4},{6,7},{7,6},{2,3},{3,2},{8,9},{9,8},{12,13... | collective-permute-start | bytes 786440 | tf_op jit(solution)/shard_map/ppermute | solution.py:418
  103.3 14.3 %collective-permute-start.30 = (bf16[256,1024]{1,0:T(8,128)(2,1)S(1)}, bf16[256,1024]{1,0:T(8,128)(2,1)S(1)}, u32[]{:S(2)}, u32[]{:S(2)}) collective-permute-start(bf16[256,1024]{1,0:T(8,128)(2,1)S(1)} %add_convert_fusion), channel_id=1, source_target_pairs={{0,4},{1,5},{4,6},{5,7},{6,2},{7,3},{2,0},{3,1},{8,12},{9,13},{12,... | collective-permute-start | bytes 1572872 | tf_op jit(solution)/shard_map/ppermute | solution.py:415
  117.8 11.2 %collective-permute-start.31 = (bf16[128,1024]{1,0:T(8,128)(2,1)S(1)}, bf16[128,1024]{1,0:T(8,128)(2,1)S(1)}, u32[]{:S(2)}, u32[]{:S(2)}) collective-permute-start(bf16[128,1024]{1,0:T(8,128)(2,1)S(1)} %add_convert_fusion.5), channel_id=1, source_target_pairs={{0,1},{1,0},{4,5},{5,4},{6,7},{7,6},{2,3},{3,2},{8,9},{9,8},{12,13... | collective-permute-start | bytes 786440 | tf_op jit(solution)/shard_map/ppermute | solution.py:536
  120.3 14.3 %collective-permute-start.40 = (bf16[128,1024]{1,0:T(8,128)(2,1)S(1)}, bf16[128,1024]{1,0:T(8,128)(2,1)S(1)}, u32[]{:S(2)}, u32[]{:S(2)}) collective-permute-start(bf16[128,1024]{1,0:T(8,128)(2,1)S(1)} %get-tuple-element.104), channel_id=1, source_target_pairs={{0,1},{1,0},{4,5},{5,4},{6,7},{7,6},{2,3},{3,2},{8,9},{9,8},{12,13... | collective-permute-start | bytes 786440 | tf_op jit(solution)/shard_map/ppermute | solution.py:536
  123.5 11.1 %collective-permute-start.39 = (bf16[128,1024]{1,0:T(8,128)(2,1)S(1)}, bf16[128,1024]{1,0:T(8,128)(2,1)S(1)}, u32[]{:S(2)}, u32[]{:S(2)}) collective-permute-start(bf16[128,1024]{1,0:T(8,128)(2,1)S(1)} %add_convert_fusion.2), channel_id=1, source_target_pairs={{0,4},{1,5},{4,6},{5,7},{6,2},{7,3},{2,0},{3,1},{8,12},{9,13},{12,... | collective-permute-start | bytes 786440 | tf_op jit(solution)/shard_map/ppermute | solution.py:415
  129.1 11.1 %collective-permute-start.32 = (bf16[128,1024]{1,0:T(8,128)(2,1)S(1)}, bf16[128,1024]{1,0:T(8,128)(2,1)S(1)}, u32[]{:S(2)}, u32[]{:S(2)}) collective-permute-start(bf16[128,1024]{1,0:T(8,128)(2,1)S(1)} %add_convert_fusion.4), channel_id=1, source_target_pairs={{0,4},{1,5},{4,6},{5,7},{6,2},{7,3},{2,0},{3,1},{8,12},{9,13},{12,... | collective-permute-start | bytes 786440 | tf_op jit(solution)/shard_map/ppermute | solution.py:415
  132.3 12.4 %collective-permute-start.42 = (bf16[128,1024]{1,0:T(8,128)(2,1)S(1)}, bf16[128,1024]{1,0:T(8,128)(2,1)S(1)}, u32[]{:S(2)}, u32[]{:S(2)}) collective-permute-start(bf16[128,1024]{1,0:T(8,128)(2,1)S(1)} %get-tuple-element.106), channel_id=1, source_target_pairs={{0,1},{1,0},{4,5},{5,4},{6,7},{7,6},{2,3},{3,2},{8,9},{9,8},{12,13... | collective-permute-start | bytes 786440 | tf_op jit(solution)/shard_map/ppermute | solution.py:536
  134.7 10.0 %collective-permute-start.41 = (bf16[128,1024]{1,0:T(8,128)(2,1)S(1)}, bf16[128,1024]{1,0:T(8,128)(2,1)S(1)}, u32[]{:S(2)}, u32[]{:S(2)}) collective-permute-start(bf16[128,1024]{1,0:T(8,128)(2,1)S(1)} %add_convert_fusion.1), channel_id=1, source_target_pairs={{0,4},{1,5},{4,6},{5,7},{6,2},{7,3},{2,0},{3,1},{8,12},{9,13},{12,... | collective-permute-start | bytes 786440 | tf_op jit(solution)/shard_map/ppermute | solution.py:415
  (26 other events, 372.1 us)

commit v3 on v2

--- a/solution.py
+++ b/solution.py
@@ -509,6 +509,8 @@
         downs += [down, other_core(down, *soon)]
 
     terms, fallen = [None] * HALVES, {}
+    fallen[2, 1] = fall(acts[2], depth_y, downs[each:])
+    chunks[final][0][0] = tie(chunks[final][0][0], fallen[2, 1][0])
     acts[final] = rise(chunks[final], gates, ups)
     fallen[final, 0] = fall(acts[final], depth_y, downs[:each])
     filler = fallen[final, 0][0]

time: 146 us -> 145 us (level)
    ppermute x12, waiting for transfers between devices: 15.6 us -> 19.9 us  [along_y(): lax.ppermute(tie(block, *others), 'dev', shift(0, ys))]
    ppermute x15, waiting for transfers between devices: 19.2 us -> 15.5 us  [round_z(): return lax.ppermute(tie(block, *others), 'dev', shift(1, 0))]
  transfers between devices with their start and end apart: 43 -> 43, of which waited for: 23 -> 24; matrix products, arithmetic and copies ran while one was open for 2% -> 2% of each run, Pallas kernels for 23% -> 23%
where the time goes in v3:
time: 145 us
  waiting for transfers between devices  53.6 us (37%)
  starting transfers between devices  52.8 us (36%)
  Pallas kernels  34 us (23%)
  other arithmetic  3.41 us (2%)
    ppermute x15, starting transfers between devices, round_z(): return lax.ppermute(tie(block, *others), 'dev', shift(1, 0))  26.7 us
    ppermute x12, waiting for transfers between devices, along_y(): lax.ppermute(tie(block, *others), 'dev', shift(0, ys))  19.9 us
    ppermute x15, waiting for transfers between devices, round_z(): return lax.ppermute(tie(block, *others), 'dev', shift(1, 0))  15.5 us
    ppermute x6, waiting for transfers between devices, shards(): lax.ppermute(parts[ys], 'dev', shift(0, -ys))  13.8 us
    ppermute x12, starting transfers between devices, along_y(): lax.ppermute(tie(block, *others), 'dev', shift(0, ys))  13.2 us
    pallas_call x4, Pallas kernels, rise(): pl.pallas_call(kernel, out_shape=jax.ShapeDtypeStruct((parts * tokens, hi...  12.3 us
    pallas_call x8, Pallas kernels, fall(): pl.pallas_call(kernel, out_shape=[shape] * parts, in_specs=[vmem] * (1 +...  9.82 us
    pallas_call x2, Pallas kernels, attend(): pl.pallas_call(kernel, out_shape=[shape] * 3, in_specs=[vmem] * len(opera...  6.84 us
  transfers between devices with their start and end apart: 43, of which 24 were waited for; matrix products, arithmetic and copies ran while one was open for 2% of the time, Pallas kernels for 23%

profile of v3, /device:TPU:0, one launch (start us, length us, event | category | flops | bytes accessed | tf_op | source)
XLA Modules:
  0.0 145.1 jit_solution(15835881825851903457)
XLA Ops:
  1.2 4.1 %collective-permute-start.2 = (bf16[2,256,256]{2,1,0:T(8,128)(2,1)S(1)}, bf16[2,256,256]{2,1,0:T(8,128)(2,1)S(1)}, u32[]{:S(2)}, u32[]{:S(2)}) collective-permute-start(bf16[2,256,256]{2,1,0:T(8,128)(2,1)S(1)} %pad_maximum_fusion.refs_5_), channel_id=1, source_target_pairs={{0,4},{1,5},{4,6},{5,7},{6,2},{7,3},{2,0},{3,1},{8,12},{9,13},{12,... | collective-permute-start | bytes 786440 | tf_op jit(solution)/shard_map/ppermute | solution.py:415
  7.6 2.4 %collective-permute-start = (bf16[2,128,256]{2,1,0:T(8,128)(2,1)S(1)}, bf16[2,128,256]{2,1,0:T(8,128)(2,1)S(1)}, u32[]{:S(2)}, u32[]{:S(2)}) collective-permute-start(bf16[2,128,256]{2,1,0:T(8,128)(2,1)S(1)} %pad_maximum_fusion.1.refs_3_), channel_id=1, source_target_pairs={{0,1},{1,2},{2,3},{3,4},{4,5},{5,6},{6,7},{8,9},{9,10},{10,11},{11... | collective-permute-start | bytes 393224 | tf_op jit(solution)/shard_map/ppermute | solution.py:437
  11.6 3.2 %collective-permute-done.refs_1_ = bf16[2,128,256]{2,1,0:T(8,128)(2,1)S(1)} collective-permute-done((bf16[2,128,256]{2,1,0:T(8,128)(2,1)S(1)}, bf16[2,128,256]{2,1,0:T(8,128)(2,1)S(1)}, u32[]{:S(2)}, u32[]{:S(2)}) %collective-permute-start) | collective-permute-done | bytes 131104 | tf_op jit(solution)/shard_map/ppermute | solution.py:437
  14.9 3.2 %collective-permute-start.4 = (bf16[2,256,256]{2,1,0:T(8,128)(2,1)S(1)}, bf16[2,256,256]{2,1,0:T(8,128)(2,1)S(1)}, u32[]{:S(2)}, u32[]{:S(2)}) collective-permute-start(bf16[2,256,256]{2,1,0:T(8,128)(2,1)S(1)} %collective-permute-done.2.refs_9_), channel_id=1, source_target_pairs={{0,4},{1,5},{4,6},{5,7},{6,2},{7,3},{2,0},{3,1},{8,12},{9,13},{12,... | collective-permute-start | bytes 786440 | tf_op jit(solution)/shard_map/ppermute | solution.py:415
  24.2 3.4 %collective-permute-start.6 = (bf16[2,256,256]{2,1,0:T(8,128)(2,1)S(1)}, bf16[2,256,256]{2,1,0:T(8,128)(2,1)S(1)}, u32[]{:S(2)}, u32[]{:S(2)}) collective-permute-start(bf16[2,256,256]{2,1,0:T(8,128)(2,1)S(1)} %collective-permute-done.4.refs_13_), channel_id=1, source_target_pairs={{0,4},{1,5},{4,6},{5,7},{6,2},{7,3},{2,0},{3,1},{8,12},{9,13},{12,... | collective-permute-start | bytes 786440 | tf_op jit(solution)/shard_map/ppermute | solution.py:415
  28.5 4.3 %attend.2 = (f32[2,512,128]{2,1,0:T(8,128)S(1)}, f32[2,512,128]{2,1,0:T(8,128)S(1)}, f32[2,512,128]{2,1,0:T(8,128)S(1)}) custom-call(bf16[2,1024,128]{2,1,0:T(8,128)(2,1)S(1)} %get-tuple-element.57.refs_0_, bf16[2,128,256]{2,1,0:T(8,128)(2,1)S(1)} %collective-permute-done.refs_1_, f32[128,128]{1,0:T(8,128)S(1)} %get-tuple-element.58.refs_2_, ...), custom_call_target="tpu_custom_call" | custom-call | bytes 26950000 | tf_op jit(solution)/shard_map/attend/pallas_call | solution.py:189
  33.0 2.2 %collective-permute-done.5.refs_4_ = bf16[2,256,256]{2,1,0:T(8,128)(2,1)S(1)} collective-permute-done((bf16[2,256,256]{2,1,0:T(8,128)(2,1)S(1)}, bf16[2,256,256]{2,1,0:T(8,128)(2,1)S(1)}, u32[]{:S(2)}, u32[]{:S(2)}) %collective-permute-start.5) | collective-permute-done | bytes 262176 | tf_op jit(solution)/shard_map/ppermute | solution.py:418
  38.1 2.5 %attend.3 = (f32[2,512,128]{2,1,0:T(8,128)S(1)}, f32[2,512,128]{2,1,0:T(8,128)S(1)}, f32[2,512,128]{2,1,0:T(8,128)S(1)}) custom-call(bf16[2,1024,128]{2,1,0:T(8,128)(2,1)S(1)} %get-tuple-element.57.refs_0_, f32[2,512,128]{2,1,0:T(8,128)S(1)} %get-tuple-element.63.refs_1_, f32[2,512,128]{2,1,0:T(8,128)S(1)} %get-tuple-element.64.refs_2_, ...), custom_call_target="tpu_custom_call" | custom-call | bytes 7700000 | tf_op jit(solution)/shard_map/attend/pallas_call | solution.py:189
  40.8 4.4 %collective-permute-done.9.refs_4_ = bf16[2,256,256]{2,1,0:T(8,128)(2,1)S(1)} collective-permute-done((bf16[2,256,256]{2,1,0:T(8,128)(2,1)S(1)}, bf16[2,256,256]{2,1,0:T(8,128)(2,1)S(1)}, u32[]{:S(2)}, u32[]{:S(2)}) %collective-permute-start.9) | collective-permute-done | bytes 262176 | tf_op jit(solution)/shard_map/ppermute | solution.py:418
  45.2 2.4 %attend_project.1 = (f32[128,2048]{1,0:T(8,128)S(1)}, bf16[128,1024]{1,0:T(8,128)(2,1)S(1)}, bf16[128,1024]{1,0:T(8,128)(2,1)S(1)}) custom-call(bf16[2,1024,128]{2,1,0:T(8,128)(2,1)S(1)} %get-tuple-element.57.refs_0_, f32[2,512,128]{2,1,0:T(8,128)S(1)} %get-tuple-element.68.refs_1_, f32[2,512,128]{2,1,0:T(8,128)S(1)} %get-tuple-element.69.refs_2_, ...), custom_call_target="tpu_custom_call" | custom-call | bytes 10850000 | tf_op jit(solution)/shard_map/attend_project/pallas_call | solution.py:252
  51.7 5.2 %collective-permute-done.16.refs_0_ = bf16[128,1024]{1,0:T(8,128)(2,1)S(1)} collective-permute-done((bf16[128,1024]{1,0:T(8,128)(2,1)S(1)}, bf16[128,1024]{1,0:T(8,128)(2,1)S(1)}, u32[]{:S(2)}, u32[]{:S(2)}) %collective-permute-start.16) | collective-permute-done | bytes 262176 | tf_op jit(solution)/shard_map/ppermute | solution.py:415
  59.1 3.5 %collective-permute-done.18.refs_1_ = bf16[128,1024]{1,0:T(8,128)(2,1)S(1)} collective-permute-done((bf16[128,1024]{1,0:T(8,128)(2,1)S(1)}, bf16[128,1024]{1,0:T(8,128)(2,1)S(1)}, u32[]{:S(2)}, u32[]{:S(2)}) %collective-permute-start.18) | collective-permute-done | bytes 262176 | tf_op jit(solution)/shard_map/ppermute | solution.py:415
  64.5 2.2 %collective-permute-start.19 = (bf16[128,1024]{1,0:T(8,128)(2,1)S(1)}, bf16[128,1024]{1,0:T(8,128)(2,1)S(1)}, u32[]{:S(2)}, u32[]{:S(2)}) collective-permute-start(bf16[128,1024]{1,0:T(8,128)(2,1)S(1)} %collective-permute-done.18.refs_1_), channel_id=1, source_target_pairs={{0,4},{1,5},{4,6},{5,7},{6,2},{7,3},{2,0},{3,1},{8,12},{9,13},{12,... | collective-permute-start | bytes 786440 | tf_op jit(solution)/shard_map/ppermute | solution.py:415
  69.8 2.8 %collective-permute-done.21.refs_3_ = bf16[128,1024]{1,0:T(8,128)(2,1)S(1)} collective-permute-done((bf16[128,1024]{1,0:T(8,128)(2,1)S(1)}, bf16[128,1024]{1,0:T(8,128)(2,1)S(1)}, u32[]{:S(2)}, u32[]{:S(2)}) %collective-permute-start.21) | collective-permute-done | bytes 262176 | tf_op jit(solution)/shard_map/ppermute | solution.py:418
  77.6 3.1 %rise.6.refs_0_ = bf16[256,1024]{1,0:T(8,128)(2,1)S(1)} custom-call(bf16[128,1024]{1,0:T(8,128)(2,1)S(1)} %collective-permute-done.16.refs_0_, bf16[128,1024]{1,0:T(8,128)(2,1)S(1)} %collective-permute-done.18.refs_1_, bf16[128,1024]{1,0:T(8,128)(2,1)S(1)} %collective-permute-done.20.refs_2_, bf16[128,1024]{1,0:T(8,128)(2,1)S(1)} %collective-permute-done.21.refs_3_, ...), custom_call_target="tpu_custom_call" | custom-call | bytes 10500000 | tf_op jit(solution)/shard_map/rise/pallas_call | solution.py:299
  83.5 4.9 %collective-permute-done.25.refs_3_ = bf16[128,1024]{1,0:T(8,128)(2,1)S(1)} collective-permute-done((bf16[128,1024]{1,0:T(8,128)(2,1)S(1)}, bf16[128,1024]{1,0:T(8,128)(2,1)S(1)}, u32[]{:S(2)}, u32[]{:S(2)}) %collective-permute-start.25) | collective-permute-done | bytes 262176 | tf_op jit(solution)/shard_map/ppermute | solution.py:418
  91.7 3.1 %rise.4.refs_0_ = bf16[256,1024]{1,0:T(8,128)(2,1)S(1)} custom-call(bf16[128,1024]{1,0:T(8,128)(2,1)S(1)} %get-tuple-element.76.refs_0_, bf16[128,1024]{1,0:T(8,128)(2,1)S(1)} %get-tuple-element.77.refs_1_, bf16[128,1024]{1,0:T(8,128)(2,1)S(1)} %collective-permute-done.13.refs_2_, bf16[128,1024]{1,0:T(8,128)(2,1)S(1)} %collective-permute-done.14.refs_3_, ...), custom_call_target="tpu_custom_call" | custom-call | bytes 10500000 | tf_op jit(solution)/shard_map/rise/pallas_call | solution.py:299
  94.7 3.1 %rise.5.refs_0_ = bf16[256,1024]{1,0:T(8,128)(2,1)S(1)} custom-call(bf16[128,1024]{1,0:T(8,128)(2,1)S(1)} %collective-permute-done.17.refs_0_, bf16[128,1024]{1,0:T(8,128)(2,1)S(1)} %collective-permute-done.19.refs_1_, bf16[128,1024]{1,0:T(8,128)(2,1)S(1)} %collective-permute-done.24.refs_2_, bf16[128,1024]{1,0:T(8,128)(2,1)S(1)} %collective-permute-done.25.refs_3_, ...), custom_call_target="tpu_custom_call" | custom-call | bytes 10500000 | tf_op jit(solution)/shard_map/rise/pallas_call | solution.py:299
  99.0 2.7 %collective-permute-done.30 = bf16[256,1024]{1,0:T(8,128)(2,1)S(1)} collective-permute-done((bf16[256,1024]{1,0:T(8,128)(2,1)S(1)}, bf16[256,1024]{1,0:T(8,128)(2,1)S(1)}, u32[]{:S(2)}, u32[]{:S(2)}) %collective-permute-start.30) | collective-permute-done | bytes 524320 | tf_op jit(solution)/shard_map/ppermute | solution.py:415
  109.1 3.1 %rise.7.refs_0_ = bf16[256,1024]{1,0:T(8,128)(2,1)S(1)} custom-call(bf16[128,1024]{1,0:T(8,128)(2,1)S(1)} %collective-permute-done.23.refs_0_, bf16[128,1024]{1,0:T(8,128)(2,1)S(1)} %collective-permute-done.27.refs_1_, bf16[128,1024]{1,0:T(8,128)(2,1)S(1)} %collective-permute-done.28.refs_2_, bf16[128,1024]{1,0:T(8,128)(2,1)S(1)} %collective-permute-done.29.refs_3_, ...), custom_call_target="tpu_custom_call" | custom-call | bytes 10500000 | tf_op jit(solution)/shard_map/rise/pallas_call | solution.py:299
  123.0 2.4 %collective-permute-start.39 = (bf16[128,1024]{1,0:T(8,128)(2,1)S(1)}, bf16[128,1024]{1,0:T(8,128)(2,1)S(1)}, u32[]{:S(2)}, u32[]{:S(2)}) collective-permute-start(bf16[128,1024]{1,0:T(8,128)(2,1)S(1)} %add_convert_fusion.2), channel_id=1, source_target_pairs={{0,4},{1,5},{4,6},{5,7},{6,2},{7,3},{2,0},{3,1},{8,12},{9,13},{12,... | collective-permute-start | bytes 786440 | tf_op jit(solution)/shard_map/ppermute | solution.py:415
  131.7 2.2 %collective-permute-done.40 = bf16[128,1024]{1,0:T(8,128)(2,1)S(1)} collective-permute-done((bf16[128,1024]{1,0:T(8,128)(2,1)S(1)}, bf16[128,1024]{1,0:T(8,128)(2,1)S(1)}, u32[]{:S(2)}, u32[]{:S(2)}) %collective-permute-start.40) | collective-permute-done | bytes 262176 | tf_op jit(solution)/shard_map/ppermute | solution.py:538
  135.3 4.2 %collective-permute-done.35.refs_2_ = bf16[128,1024]{1,0:T(8,128)(2,1)S(1)} collective-permute-done((bf16[128,1024]{1,0:T(8,128)(2,1)S(1)}, bf16[128,1024]{1,0:T(8,128)(2,1)S(1)}, u32[]{:S(2)}, u32[]{:S(2)}) %collective-permute-start.35) | collective-permute-done | bytes 262176 | tf_op jit(solution)/shard_map/ppermute | solution.py:538
  139.5 4.5 %collective-permute-done.42.refs_5_ = bf16[128,1024]{1,0:T(8,128)(2,1)S(1)} collective-permute-done((bf16[128,1024]{1,0:T(8,128)(2,1)S(1)}, bf16[128,1024]{1,0:T(8,128)(2,1)S(1)}, u32[]{:S(2)}, u32[]{:S(2)}) %collective-permute-start.42) | collective-permute-done | bytes 262176 | tf_op jit(solution)/shard_map/ppermute | solution.py:538
  (102 shorter events, 65.9 us)
Async XLA Ops:
  1.2 13.7 %collective-permute-start.2 = (bf16[2,256,256]{2,1,0:T(8,128)(2,1)S(1)}, bf16[2,256,256]{2,1,0:T(8,128)(2,1)S(1)}, u32[]{:S(2)}, u32[]{:S(2)}) collective-permute-start(bf16[2,256,256]{2,1,0:T(8,128)(2,1)S(1)} %pad_maximum_fusion.refs_5_), channel_id=1, source_target_pairs={{0,4},{1,5},{4,6},{5,7},{6,2},{7,3},{2,0},{3,1},{8,12},{9,13},{12,... | collective-permute-start | bytes 786440 | tf_op jit(solution)/shard_map/ppermute | solution.py:415
  5.2 9.6 %collective-permute-start.1 = (bf16[2,256,256]{2,1,0:T(8,128)(2,1)S(1)}, bf16[2,256,256]{2,1,0:T(8,128)(2,1)S(1)}, u32[]{:S(2)}, u32[]{:S(2)}) collective-permute-start(bf16[2,256,256]{2,1,0:T(8,128)(2,1)S(1)} %pad_maximum_fusion.refs_5_), channel_id=1, source_target_pairs={{0,1},{1,0},{4,5},{5,4},{6,7},{7,6},{2,3},{3,2},{8,9},{9,8},{12,13... | collective-permute-start | bytes 786440 | tf_op jit(solution)/shard_map/ppermute | solution.py:418
  10.1 25.1 %collective-permute-start.8 = (bf16[512,1024]{1,0:T(8,128)(2,1)}, bf16[512,1024]{1,0:T(8,128)(2,1)S(1)}, u32[]{:S(2)}, u32[]{:S(2)}) collective-permute-start(bf16[512,1024]{1,0:T(8,128)(2,1)} %refs_4_.7), channel_id=1, source_target_pairs={{0,16},{8,24},{16,0},{24,8},{1,17},{9,25},{17,1},{25,9},{2,18},{10... | collective-permute-start | bytes 3145736 | tf_op jit(solution)/shard_map/ppermute | solution.py:423
  14.9 20.3 %collective-permute-start.7 = (bf16[512,1024]{1,0:T(8,128)(2,1)}, bf16[512,1024]{1,0:T(8,128)(2,1)S(1)}, u32[]{:S(2)}, u32[]{:S(2)}) collective-permute-start(bf16[512,1024]{1,0:T(8,128)(2,1)} %refs_4_.7), channel_id=1, source_target_pairs={{0,8},{8,0},{16,24},{24,16},{1,9},{9,1},{17,25},{25,17},{2,10},{10... | collective-permute-start | bytes 3145736 | tf_op jit(solution)/shard_map/ppermute | solution.py:427
  18.7 9.8 %collective-permute-start.3 = (bf16[2,256,256]{2,1,0:T(8,128)(2,1)S(1)}, bf16[2,256,256]{2,1,0:T(8,128)(2,1)S(1)}, u32[]{:S(2)}, u32[]{:S(2)}) collective-permute-start(bf16[2,256,256]{2,1,0:T(8,128)(2,1)S(1)} %collective-permute-done.2.refs_9_), channel_id=1, source_target_pairs={{0,1},{1,0},{4,5},{5,4},{6,7},{7,6},{2,3},{3,2},{8,9},{9,8},{12,13... | collective-permute-start | bytes 786440 | tf_op jit(solution)/shard_map/ppermute | solution.py:418
  28.5 12.2 %collective-permute-start.10 = (bf16[512,1024]{1,0:T(8,128)(2,1)}, bf16[512,1024]{1,0:T(8,128)(2,1)S(1)}, u32[]{:S(2)}, u32[]{:S(2)}) collective-permute-start(bf16[512,1024]{1,0:T(8,128)(2,1)} %refs_8_.7), channel_id=1, source_target_pairs={{0,8},{8,0},{16,24},{24,16},{1,9},{9,1},{17,25},{25,17},{2,10},{10... | collective-permute-start | bytes 3145736 | tf_op jit(solution)/shard_map/ppermute | solution.py:427
  35.7 31.0 %collective-permute-start.15 = (bf16[512,1024]{1,0:T(8,128)(2,1)}, bf16[512,1024]{1,0:T(8,128)(2,1)S(1)}, u32[]{:S(2)}, u32[]{:S(2)}) collective-permute-start(bf16[512,1024]{1,0:T(8,128)(2,1)} %refs_8_.7), channel_id=1, source_target_pairs={{0,16},{8,24},{16,0},{24,8},{1,17},{9,25},{17,1},{25,9},{2,18},{10... | collective-permute-start | bytes 3145736 | tf_op jit(solution)/shard_map/ppermute | solution.py:423
  49.9 12.6 %collective-permute-start.18 = (bf16[128,1024]{1,0:T(8,128)(2,1)S(1)}, bf16[128,1024]{1,0:T(8,128)(2,1)S(1)}, u32[]{:S(2)}, u32[]{:S(2)}) collective-permute-start(bf16[128,1024]{1,0:T(8,128)(2,1)S(1)} %get-tuple-element.77.refs_1_), channel_id=1, source_target_pairs={{0,4},{1,5},{4,6},{5,7},{6,2},{7,3},{2,0},{3,1},{8,12},{9,13},{12,... | collective-permute-start | bytes 786440 | tf_op jit(solution)/shard_map/ppermute | solution.py:415
  50.0 14.6 %collective-permute-start.14 = (bf16[128,1024]{1,0:T(8,128)(2,1)S(1)}, bf16[128,1024]{1,0:T(8,128)(2,1)S(1)}, u32[]{:S(2)}, u32[]{:S(2)}) collective-permute-start(bf16[128,1024]{1,0:T(8,128)(2,1)S(1)} %get-tuple-element.77.refs_1_), channel_id=1, source_target_pairs={{0,1},{1,0},{4,5},{5,4},{6,7},{7,6},{2,3},{3,2},{8,9},{9,8},{12,13... | collective-permute-start | bytes 786440 | tf_op jit(solution)/shard_map/ppermute | solution.py:418
  58.2 10.0 %collective-permute-start.17 = (bf16[128,1024]{1,0:T(8,128)(2,1)S(1)}, bf16[128,1024]{1,0:T(8,128)(2,1)S(1)}, u32[]{:S(2)}, u32[]{:S(2)}) collective-permute-start(bf16[128,1024]{1,0:T(8,128)(2,1)S(1)} %collective-permute-done.16.refs_0_), channel_id=1, source_target_pairs={{0,4},{1,5},{4,6},{5,7},{6,2},{7,3},{2,0},{3,1},{8,12},{9,13},{12,... | collective-permute-start | bytes 786440 | tf_op jit(solution)/shard_map/ppermute | solution.py:415
  75.4 13.1 %collective-permute-start.25 = (bf16[128,1024]{1,0:T(8,128)(2,1)S(1)}, bf16[128,1024]{1,0:T(8,128)(2,1)S(1)}, u32[]{:S(2)}, u32[]{:S(2)}) collective-permute-start(bf16[128,1024]{1,0:T(8,128)(2,1)S(1)} %collective-permute-done.19.refs_1_), channel_id=1, source_target_pairs={{0,1},{1,0},{4,5},{5,4},{6,7},{7,6},{2,3},{3,2},{8,9},{9,8},{12,13... | collective-permute-start | bytes 786440 | tf_op jit(solution)/shard_map/ppermute | solution.py:418
  76.4 12.0 %collective-permute-start.27 = (bf16[128,1024]{1,0:T(8,128)(2,1)S(1)}, bf16[128,1024]{1,0:T(8,128)(2,1)S(1)}, u32[]{:S(2)}, u32[]{:S(2)}) collective-permute-start(bf16[128,1024]{1,0:T(8,128)(2,1)S(1)} %collective-permute-done.19.refs_1_), channel_id=1, source_target_pairs={{0,4},{1,5},{4,6},{5,7},{6,2},{7,3},{2,0},{3,1},{8,12},{9,13},{12,... | collective-permute-start | bytes 786440 | tf_op jit(solution)/shard_map/ppermute | solution.py:415
  77.0 24.9 %collective-permute-start.26 = (bf16[1024,512]{1,0:T(8,128)(2,1)S(1)}, bf16[1024,512]{1,0:T(8,128)(2,1)S(1)}, u32[]{:S(2)}, u32[]{:S(2)}) collective-permute-start(bf16[1024,512]{1,0:T(8,128)(2,1)S(1)} %copy-done.2), channel_id=1, source_target_pairs={{0,16},{8,24},{16,0},{24,8},{1,17},{9,25},{17,1},{25,9},{2,18},{10... | collective-permute-start | bytes 3145736 | tf_op jit(solution)/shard_map/ppermute | solution.py:423
  88.5 13.2 %collective-permute-start.30 = (bf16[256,1024]{1,0:T(8,128)(2,1)S(1)}, bf16[256,1024]{1,0:T(8,128)(2,1)S(1)}, u32[]{:S(2)}, u32[]{:S(2)}) collective-permute-start(bf16[256,1024]{1,0:T(8,128)(2,1)S(1)} %fall.10), channel_id=1, source_target_pairs={{0,4},{1,5},{4,6},{5,7},{6,2},{7,3},{2,0},{3,1},{8,12},{9,13},{12,... | collective-permute-start | bytes 1572872 | tf_op jit(solution)/shard_map/ppermute | solution.py:415
  89.6 12.3 %collective-permute-start.28 = (bf16[128,1024]{1,0:T(8,128)(2,1)S(1)}, bf16[128,1024]{1,0:T(8,128)(2,1)S(1)}, u32[]{:S(2)}, u32[]{:S(2)}) collective-permute-start(bf16[128,1024]{1,0:T(8,128)(2,1)S(1)} %collective-permute-done.23.refs_0_), channel_id=1, source_target_pairs={{0,1},{1,0},{4,5},{5,4},{6,7},{7,6},{2,3},{3,2},{8,9},{9,8},{12,13... | collective-permute-start | bytes 786440 | tf_op jit(solution)/shard_map/ppermute | solution.py:418
  90.6 12.3 %collective-permute-start.29 = (bf16[128,1024]{1,0:T(8,128)(2,1)S(1)}, bf16[128,1024]{1,0:T(8,128)(2,1)S(1)}, u32[]{:S(2)}, u32[]{:S(2)}) collective-permute-start(bf16[128,1024]{1,0:T(8,128)(2,1)S(1)} %collective-permute-done.27.refs_1_), channel_id=1, source_target_pairs={{0,1},{1,0},{4,5},{5,4},{6,7},{7,6},{2,3},{3,2},{8,9},{9,8},{12,13... | collective-permute-start | bytes 786440 | tf_op jit(solution)/shard_map/ppermute | solution.py:418
  102.9 14.3 %collective-permute-start.32 = (bf16[256,1024]{1,0:T(8,128)(2,1)S(1)}, bf16[256,1024]{1,0:T(8,128)(2,1)S(1)}, u32[]{:S(2)}, u32[]{:S(2)}) collective-permute-start(bf16[256,1024]{1,0:T(8,128)(2,1)S(1)} %add_convert_fusion), channel_id=1, source_target_pairs={{0,4},{1,5},{4,6},{5,7},{6,2},{7,3},{2,0},{3,1},{8,12},{9,13},{12,... | collective-permute-start | bytes 1572872 | tf_op jit(solution)/shard_map/ppermute | solution.py:415
  117.3 10.9 %collective-permute-start.33 = (bf16[128,1024]{1,0:T(8,128)(2,1)S(1)}, bf16[128,1024]{1,0:T(8,128)(2,1)S(1)}, u32[]{:S(2)}, u32[]{:S(2)}) collective-permute-start(bf16[128,1024]{1,0:T(8,128)(2,1)S(1)} %add_convert_fusion.5), channel_id=1, source_target_pairs={{0,1},{1,0},{4,5},{5,4},{6,7},{7,6},{2,3},{3,2},{8,9},{9,8},{12,13... | collective-permute-start | bytes 786440 | tf_op jit(solution)/shard_map/ppermute | solution.py:538
  119.6 14.3 %collective-permute-start.40 = (bf16[128,1024]{1,0:T(8,128)(2,1)S(1)}, bf16[128,1024]{1,0:T(8,128)(2,1)S(1)}, u32[]{:S(2)}, u32[]{:S(2)}) collective-permute-start(bf16[128,1024]{1,0:T(8,128)(2,1)S(1)} %get-tuple-element.106), channel_id=1, source_target_pairs={{0,1},{1,0},{4,5},{5,4},{6,7},{7,6},{2,3},{3,2},{8,9},{9,8},{12,13... | collective-permute-start | bytes 786440 | tf_op jit(solution)/shard_map/ppermute | solution.py:538
  123.0 10.9 %collective-permute-start.39 = (bf16[128,1024]{1,0:T(8,128)(2,1)S(1)}, bf16[128,1024]{1,0:T(8,128)(2,1)S(1)}, u32[]{:S(2)}, u32[]{:S(2)}) collective-permute-start(bf16[128,1024]{1,0:T(8,128)(2,1)S(1)} %add_convert_fusion.2), channel_id=1, source_target_pairs={{0,4},{1,5},{4,6},{5,7},{6,2},{7,3},{2,0},{3,1},{8,12},{9,13},{12,... | collective-permute-start | bytes 786440 | tf_op jit(solution)/shard_map/ppermute | solution.py:415
  128.4 15.6 %collective-permute-start.34 = (bf16[128,1024]{1,0:T(8,128)(2,1)S(1)}, bf16[128,1024]{1,0:T(8,128)(2,1)S(1)}, u32[]{:S(2)}, u32[]{:S(2)}) collective-permute-start(bf16[128,1024]{1,0:T(8,128)(2,1)S(1)} %add_convert_fusion.4), channel_id=1, source_target_pairs={{0,4},{1,5},{4,6},{5,7},{6,2},{7,3},{2,0},{3,1},{8,12},{9,13},{12,... | collective-permute-start | bytes 786440 | tf_op jit(solution)/shard_map/ppermute | solution.py:415
  129.7 9.8 %collective-permute-start.35 = (bf16[128,1024]{1,0:T(8,128)(2,1)S(1)}, bf16[128,1024]{1,0:T(8,128)(2,1)S(1)}, u32[]{:S(2)}, u32[]{:S(2)}) collective-permute-start(bf16[128,1024]{1,0:T(8,128)(2,1)S(1)} %get-tuple-element.99), channel_id=1, source_target_pairs={{0,1},{1,0},{4,5},{5,4},{6,7},{7,6},{2,3},{3,2},{8,9},{9,8},{12,13... | collective-permute-start | bytes 786440 | tf_op jit(solution)/shard_map/ppermute | solution.py:538
  130.9 13.1 %collective-permute-start.42 = (bf16[128,1024]{1,0:T(8,128)(2,1)S(1)}, bf16[128,1024]{1,0:T(8,128)(2,1)S(1)}, u32[]{:S(2)}, u32[]{:S(2)}) collective-permute-start(bf16[128,1024]{1,0:T(8,128)(2,1)S(1)} %get-tuple-element.108), channel_id=1, source_target_pairs={{0,1},{1,0},{4,5},{5,4},{6,7},{7,6},{2,3},{3,2},{8,9},{9,8},{12,13... | collective-permute-start | bytes 786440 | tf_op jit(solution)/shard_map/ppermute | solution.py:538
  134.0 10.0 %collective-permute-start.41 = (bf16[128,1024]{1,0:T(8,128)(2,1)S(1)}, bf16[128,1024]{1,0:T(8,128)(2,1)S(1)}, u32[]{:S(2)}, u32[]{:S(2)}) collective-permute-start(bf16[128,1024]{1,0:T(8,128)(2,1)S(1)} %add_convert_fusion.1), channel_id=1, source_target_pairs={{0,4},{1,5},{4,6},{5,7},{6,2},{7,3},{2,0},{3,1},{8,12},{9,13},{12,... | collective-permute-start | bytes 786440 | tf_op jit(solution)/shard_map/ppermute | solution.py:415
  (26 other events, 371.6 us)
